TPU v7x, 256 devices: a whole 4x4x8 slice. The times are simulated.
256 devices in a mesh: dp: 8 (over y, core), expert: 32 (over z, x).
Axes of the slice: x: 4, y: 4, z: 8, core: 2. Of those that a mesh axis runs over, the one named last changes fastest.
Arguments:
- tokens: bfloat16 [32768, 1280], P(('dp', 'expert')), may hold values from -6 to 6
- grad_out: bfloat16 [32768, 1280], P(('dp', 'expert')), may hold values from -6 to 6
- gate: bfloat16 [32768], P(('dp', 'expert')), may hold values from 0.19921875 to 1
- expert_ids: int32 [32768, 1], P(('dp', 'expert')), may hold values from 0 to 31; in each aligned block of 128 rows (0 to 127, 128 to 255, ...) at most 6 rows name the same one
- modality: int32 [32768], P(('dp', 'expert')), may hold values 0 or 1
- modal_gain: float32 [2, 1280], replicated, may hold values from 0.5 to 2
- w_in: bfloat16 [32, 1280, 5120], P('expert', None, 'dp'), may hold values from -0.15625 to 0.15625
- w_out: bfloat16 [32, 5120, 1280], P('expert', 'dp'), may hold values from -0.078125 to 0.078125
Outputs:
- grad_tokens: bfloat16 [32768, 1280], P(('dp', 'expert'))
- grad_gate: bfloat16 [32768], P(('dp', 'expert'))
- grad_w_in: bfloat16 [32, 1280, 5120], P('expert', None, 'dp')
- grad_w_out: bfloat16 [32, 5120, 1280], P('expert', 'dp')
Inputs may be any that keep to these rules, and one draw needn't show every extreme that they name: `expert_ids`: in each aligned block of 128 tokens (the tokens of one device) no expert is named more than 6 times, a bound that some block reaches.
All inputs are finite; a program needn't handle non-finite values. No bound on the sum of `modality` on one device may be relied on, other than what follows from the above.
Results may differ from a plain program's by a relative error of at most 0.017.
Values may be sent and summed in bfloat16 or wider, within the bound.
A program may use at most 128 MiB of HBM per device.

v0:
```python
import jax
import jax.numpy as jnp
from jax import lax
from jax.sharding import PartitionSpec as P

inv_root_two = 0.7071067811865476
inv_root_two_pi = 0.3989422804014327


def gelu_parts(pre_act):
    normal_cdf = 0.5 * (1.0 + jax.scipy.special.erf(pre_act * inv_root_two))
    density = jnp.exp(-0.5 * pre_act * pre_act) * inv_root_two_pi
    return (pre_act * normal_cdf, normal_cdf + pre_act * density)


def expert_backward(rows_in, rows_grad, rows_gate, weight_in, weight_out):
    lead_shape = rows_gate.shape
    model_width = rows_in.shape[-1]
    flat_in = rows_in.reshape(-1, model_width)
    flat_grad = rows_grad.reshape(-1, model_width)
    flat_gate = rows_gate.reshape(-1).astype(jnp.float32)
    pre_act = jnp.dot(flat_in, weight_in, preferred_element_type=jnp.float32)
    activation, slope = gelu_parts(pre_act)
    held_act = (flat_gate[:, None] * activation).astype(jnp.bfloat16)
    out_grads = lax.dot_general(
        held_act, flat_grad, (((0,), (0,)), ((), ())), preferred_element_type=jnp.float32
    )
    back_grad = lax.dot_general(
        flat_grad, weight_out, (((1,), (1,)), ((), ())), preferred_element_type=jnp.float32
    )
    gate_part = jnp.sum(activation * back_grad, axis=1)
    pre_grad = (flat_gate[:, None] * back_grad * slope).astype(jnp.bfloat16)
    in_grads = lax.dot_general(
        flat_in, pre_grad, (((0,), (0,)), ((), ())), preferred_element_type=jnp.float32
    )
    token_part = lax.dot_general(
        pre_grad, weight_in, (((1,), (1,)), ((), ())), preferred_element_type=jnp.float32
    )
    return (
        token_part.reshape(lead_shape + (model_width,)),
        gate_part.reshape(lead_shape),
        in_grads.astype(jnp.bfloat16),
        out_grads.astype(jnp.bfloat16),
    )


def local(tokens, grad_out, gate, expert_ids, modality, modal_gain, w_in, w_out):
    experts = lax.axis_size("expert")
    tok_rows = tokens.shape[0]
    model_width = tokens.shape[1]
    capacity = 3 * tok_rows // (2 * experts)
    chosen = expert_ids[:, 0]
    onehot = (chosen[:, None] == jnp.arange(experts, dtype=jnp.int32)[None, :]).astype(jnp.int32)
    before = jnp.cumsum(onehot, axis=0) - onehot
    slot_pos = jnp.sum(before * onehot, axis=1)
    target = chosen * capacity + slot_pos
    select = (jnp.arange(experts * capacity, dtype=jnp.int32)[:, None] == target[None, :]).astype(
        jnp.bfloat16
    )
    gain_rows = jnp.where(modality[:, None] == 1, modal_gain[1][None, :], modal_gain[0][None, :])
    scaled = (gain_rows * grad_out.astype(jnp.float32)).astype(jnp.bfloat16)
    send_in = jnp.dot(select, tokens, preferred_element_type=jnp.float32).astype(jnp.bfloat16)
    send_grad = jnp.dot(select, scaled, preferred_element_type=jnp.float32).astype(jnp.bfloat16)
    send_gate = jnp.dot(select, gate[:, None], preferred_element_type=jnp.float32).astype(
        jnp.bfloat16
    )
    send_in = send_in.reshape(experts, capacity, model_width)
    send_grad = send_grad.reshape(experts, capacity, model_width)
    send_gate = send_gate.reshape(experts, capacity)
    weight_in = w_in[0]
    weight_out = w_out[0]
    col_in, col_grad, col_gate = (
        lax.all_gather(send_in[None], "dp", axis=0, tiled=True),
        lax.all_gather(send_grad[None], "dp", axis=0, tiled=True),
        lax.all_gather(send_gate[None], "dp", axis=0, tiled=True),
    )
    rows_in, rows_grad, rows_gate = (
        lax.all_to_all(col_in, "expert", split_axis=1, concat_axis=1, tiled=True),
        lax.all_to_all(col_grad, "expert", split_axis=1, concat_axis=1, tiled=True),
        lax.all_to_all(col_gate, "expert", split_axis=1, concat_axis=1, tiled=True),
    )
    token_part, gate_part, in_grads, out_grads = expert_backward(
        rows_in, rows_grad, rows_gate, weight_in, weight_out
    )
    back_tok, back_gate = (
        lax.all_to_all(
            token_part.astype(jnp.bfloat16), "expert", split_axis=1, concat_axis=1, tiled=True
        ),
        lax.all_to_all(
            gate_part.astype(jnp.bfloat16), "expert", split_axis=1, concat_axis=1, tiled=True
        ),
    )
    summed_tok, summed_gate = (
        lax.psum_scatter(back_tok, "dp", scatter_dimension=0, tiled=True).astype(jnp.float32),
        lax.psum_scatter(back_gate, "dp", scatter_dimension=0, tiled=True).astype(jnp.float32),
    )
    home_tok = summed_tok[0].astype(jnp.bfloat16)
    home_gate = summed_gate[0].astype(jnp.bfloat16)
    flat_tok = home_tok.reshape(experts * capacity, model_width)
    flat_gate = home_gate.reshape(experts * capacity, 1)
    grad_tokens = lax.dot_general(
        select, flat_tok, (((0,), (0,)), ((), ())), preferred_element_type=jnp.float32
    )
    grad_gate = lax.dot_general(
        select, flat_gate, (((0,), (0,)), ((), ())), preferred_element_type=jnp.float32
    )
    return (
        grad_tokens.astype(jnp.bfloat16),
        grad_gate[:, 0].astype(jnp.bfloat16),
        in_grads[None],
        out_grads[None],
    )


def solution(mesh):
    placed = (
        P(("dp", "expert"), None),
        P(("dp", "expert"), None),
        P(("dp", "expert")),
        P(("dp", "expert"), None),
        P(("dp", "expert")),
        P(),
        P("expert", None, "dp"),
        P("expert", "dp", None),
    )
    return jax.shard_map(
        local,
        mesh=mesh,
        in_specs=placed,
        out_specs=(
            P(("dp", "expert"), None),
            P(("dp", "expert")),
            P("expert", None, "dp"),
            P("expert", "dp", None),
        ),
        check_vma=False,
    )
```

profile of v0, /device:TPU:96, one launch (start us, length us, event | category | flops | bytes accessed | tf_op | source)
XLA Modules:
  0.0 438.4 jit_solution(11087225800681030615)
XLA Ops:
  7.2 0.8 fusion.21
  8.1 0.2 reduce_window_sum.11
  8.3 0.8 select_reduce_fusion
  9.1 0.7 multiply_add_fusion
  9.8 1.2 convolution_convert_fusion.3
  11.0 0.2 broadcast_in_dim_reshape.11
  11.2 0.9 copy.50
  12.1 0.8 fusion.20
  13.1 12.1 %all_gather.9 = bf16[8,32,6]{1,2,0:T(8,128)(2,1)S(1)} all-gather(bf16[1,32,6]{1,2,0:T(8,128)(2,1)S(1)} %copy.43), channel_id=1, replica_groups=mesh['dp'=8,'expert'=32] {'dp'}, dimensions={0}, use_global_device_ids=true | all-gather | bytes 3456 | tf_op jit(solution)/shard_map/all_gather | solution.py:75
  25.2 0.8 copy.44
  26.0 10.3 %all-to-all-start = ((bf16[8,32,6]{2,0,1:T(8,128)(2,1)}), bf16[8,32,6]{2,0,1:T(8,128)(2,1)S(1)}, u32[]{:S(2)}, u32[]{:S(2)}) async-start(bf16[8,32,6]{2,0,1:T(8,128)(2,1)} %copy.44), calls=%async_computation | async-start | bytes 131072 | tf_op jit(solution)/shard_map/all_to_all | solution.py:80
  36.3 11.4 %all-gather.5.cloned.1.call-done = bf16[8,32,6,1280]{3,1,2,0:T(8,128)(2,1)} async-done(((bf16[1,32,6,1280]{3,1,2,0:T(8,128)(2,1)}), bf16[8,32,6,1280]{3,1,2,0:T(8,128)(2,1)}) %all-gather.5.cloned.1.call-update) | async-done | bytes 3932176 | tf_op jit(solution)/shard_map/all_gather | solution.py:73
  47.7 6.2 %copy.51 = bf16[8,32,6,1280]{3,0,2,1:T(8,128)(2,1)} copy(bf16[8,32,6,1280]{3,1,2,0:T(8,128)(2,1)} %all-gather.5.cloned.1.call-done) | data formatting | bytes 7864320 | tf_op jit(solution)/shard_map/all_gather | solution.py:73
  54.0 10.1 %all-to-all-start.2 = ((bf16[8,32,6,1280]{3,0,2,1:T(8,128)(2,1)}), bf16[8,32,6,1280]{3,0,2,1:T(8,128)(2,1)}, u32[]{:S(2)}, u32[]{:S(2)}) async-start(bf16[8,32,6,1280]{3,0,2,1:T(8,128)(2,1)} %copy.51), calls=%async_computation.2 | async-start | bytes 7864320 | tf_op jit(solution)/shard_map/all_to_all | solution.py:78
  64.2 0.4 convolution_convert_fusion.4
  64.5 0.2 broadcast_in_dim_reshape.10
  64.7 0.9 copy.47
  65.6 35.2 %all-gather.3.cloned.1.call-done = bf16[8,32,6,1280]{3,1,2,0:T(8,128)(2,1)} async-done(((bf16[1,32,6,1280]{3,1,2,0:T(8,128)(2,1)}), bf16[8,32,6,1280]{3,1,2,0:T(8,128)(2,1)}) %all-gather.3.cloned.1.call-update) | async-done | bytes 3932176 | tf_op jit(solution)/shard_map/all_gather | solution.py:74
  100.8 6.1 %copy.48 = bf16[8,32,6,1280]{3,0,2,1:T(8,128)(2,1)} copy(bf16[8,32,6,1280]{3,1,2,0:T(8,128)(2,1)} %all-gather.3.cloned.1.call-done) | data formatting | bytes 7864320 | tf_op jit(solution)/shard_map/all_gather | solution.py:74
  106.9 43.8 %all-to-all-done.2 = bf16[8,32,6,1280]{3,0,2,1:T(8,128)(2,1)} async-done(((bf16[8,32,6,1280]{3,0,2,1:T(8,128)(2,1)}), bf16[8,32,6,1280]{3,0,2,1:T(8,128)(2,1)}, u32[]{:S(2)}, u32[]{:S(2)}) %all-to-all-start.2) | async-done | bytes 3932192 | tf_op jit(solution)/shard_map/all_to_all | solution.py:78
  150.7 9.6 %all-to-all-start.1 = ((bf16[8,32,6,1280]{3,0,2,1:T(8,128)(2,1)}), bf16[8,32,6,1280]{3,0,2,1:T(8,128)(2,1)}, u32[]{:S(2)}, u32[]{:S(2)}) async-start(bf16[8,32,6,1280]{3,0,2,1:T(8,128)(2,1)} %copy.48), calls=%async_computation.1 | async-start | bytes 7864320 | tf_op jit(solution)/shard_map/all_to_all | solution.py:79
  160.4 0.2 reduce-scatter.2.cloned.1.call-start
  160.6 0.1 copy.45
  161.0 5.4 %copy.52 = bf16[8,32,6,1280]{3,2,1,0:T(8,128)(2,1)} copy(bf16[8,32,6,1280]{3,0,2,1:T(8,128)(2,1)} %all-to-all-done.2) | data formatting | bytes 7864320 | tf_op jit(solution)/shard_map/all_to_all | solution.py:78
  166.4 7.2 %reshape.52 = bf16[1536,1280]{1,0:T(8,128)(2,1)} reshape(bf16[8,32,6,1280]{3,2,1,0:T(8,128)(2,1)} %copy.52) | data formatting | bytes 7864320 | tf_op jit(solution)/shard_map/reshape | solution.py:19
  173.6 73.2 %all-to-all-done.1 = bf16[8,32,6,1280]{3,0,2,1:T(8,128)(2,1)} async-done(((bf16[8,32,6,1280]{3,0,2,1:T(8,128)(2,1)}), bf16[8,32,6,1280]{3,0,2,1:T(8,128)(2,1)}, u32[]{:S(2)}, u32[]{:S(2)}) %all-to-all-start.1) | async-done | bytes 3932192 | tf_op jit(solution)/shard_map/all_to_all | solution.py:79
  246.8 5.4 %copy.49 = bf16[8,32,6,1280]{3,2,1,0:T(8,128)(2,1)} copy(bf16[8,32,6,1280]{3,0,2,1:T(8,128)(2,1)} %all-to-all-done.1) | data formatting | bytes 7864320 | tf_op jit(solution)/shard_map/all_to_all | solution.py:79
  252.2 7.2 %reshape.51 = bf16[1536,1280]{1,0:T(8,128)(2,1)} reshape(bf16[8,32,6,1280]{3,2,1,0:T(8,128)(2,1)} %copy.49) | data formatting | bytes 7864320 | tf_op jit(solution)/shard_map/reshape | solution.py:20
  259.5 5.5 %fusion.12 = f32[1536,640]{1,0:T(8,128)S(1)} fusion(bf16[1536,1280]{1,0:T(8,128)(2,1)} %reshape.52, bf16[1,1280,640]{2,1,0:T(8,128)(2,1)S(1)} %copy-done), kind=kOutput, calls=%fused_computation.22 | convolution fusion | flops 2516582400 | bytes 9502720 | tf_op jit(solution)/shard_map/dot_general | solution.py:22
  265.0 5.5 %multiply_reduce_fusion = (bf16[1536]{0:T(1024)(128)(2,1)S(1)}, bf16[1536,640]{1,0:T(8,128)(2,1)}) fusion(f32[1536,640]{1,0:T(8,128)S(1)} %fusion.12, f32[1536]{0:T(1024)S(1)} %reshape.53, bf16[1536,1280]{1,0:T(8,128)(2,1)S(1)} %copy-done.2, bf16[1,640,1280]{2,1,0:T(8,128)(2,1)S(1)} %copy-done.6), kind=kOutput, calls=%fused_computation.9 | convolution fusion | flops 2530343424 | bytes 11478016 | tf_op jit(solution)/shard_map/dot_general | solution.py:28
  270.4 4.5 %dot_general.37 = bf16[8,32,6,640]{3,2,1,0:T(8,128)(2,1)} reshape(bf16[1536,640]{1,0:T(8,128)(2,1)} %get-tuple-element.7) | data formatting | bytes 3932160 | tf_op jit(solution)/shard_map/dot_general | solution.py:36
  274.9 5.0 %convolution_convert_fusion = bf16[8,32,6,1280]{3,1,2,0:T(8,128)(2,1)S(1)} fusion(bf16[8,32,6,640]{3,2,1,0:T(8,128)(2,1)} %dot_general.37, bf16[1,1280,640]{2,1,0:T(8,128)(2,1)S(1)} %copy-done), kind=kOutput, calls=%fused_computation.1 | convolution fusion | flops 2518548480 | bytes 7536640 | tf_op jit(solution)/shard_map/dot_general | solution.py:36
  279.9 2.2 copy.54
  282.1 98.1 %all_to_all.25 = bf16[8,32,6,1280]{3,0,2,1:T(8,128)(2,1)S(1)} all-to-all(bf16[8,32,6,1280]{3,0,2,1:T(8,128)(2,1)S(1)} %copy.54), channel_id=1, replica_groups=mesh['dp'=8,'expert'=32] {'expert'}, dimensions={1} | all-to-all | bytes 7864320 | tf_op jit(solution)/shard_map/all_to_all | solution.py:86
  380.2 3.1 copy.55
  383.3 0.6 copy-done.8
  383.9 0.6 dynamic-slice
  384.5 0.2 convert_element_type.83
  384.7 0.7 copy.57
  385.3 6.6 %all-to-all-start.4 = ((bf16[8,32,6]{2,0,1:T(8,128)(2,1)}), bf16[8,32,6]{2,0,1:T(8,128)(2,1)S(1)}, u32[]{:S(2)}, u32[]{:S(2)}) async-start(bf16[8,32,6]{2,0,1:T(8,128)(2,1)} %copy.57), calls=%async_computation.5 | async-start | bytes 131072 | tf_op jit(solution)/shard_map/all_to_all | solution.py:89
  392.0 7.7 %fusion.7 = bf16[1,640,1280]{2,1,0:T(8,128)(2,1)} fusion(bf16[1536,1280]{1,0:T(8,128)(2,1)} %reshape.51, f32[1536]{0:T(1024)S(1)} %reshape.53, f32[1536,640]{1,0:T(8,128)} %copy-done.9), kind=kOutput, calls=%fused_computation.14 | convolution fusion | flops 2523299840 | bytes 9508864 | tf_op jit(solution)/shard_map/dot_general | solution.py:25
  399.6 4.4 %fusion.6 = bf16[1,1280,640]{2,1,0:T(8,128)(2,1)} fusion(bf16[1536,1280]{1,0:T(8,128)(2,1)S(1)} %copy-done.1, bf16[1536,640]{1,0:T(8,128)(2,1)S(1)} %copy-done.3), kind=kOutput, calls=%fused_computation.13 | convolution fusion | flops 2517401600 | bytes 7536640 | tf_op jit(solution)/shard_map/dot_general | solution.py:33
  404.2 23.7 %all-reduce = bf16[8,32,6]{1,2,0:T(8,128)(2,1)S(1)} all-reduce(bf16[8,32,6]{1,2,0:T(8,128)(2,1)S(1)} %copy.58), channel_id=3, replica_groups=mesh['dp'=8,'expert'=32] {'dp'}, use_global_device_ids=true, to_apply=%region_4.5.clone | all-reduce | flops 1536 | bytes 6144
  427.8 0.6 constant_dynamic-slice_fusion
  428.7 0.7 fusion.16
  429.4 1.3 copy.56
  430.7 0.2 convert_element_type.80
  430.9 1.0 convolution_convert_fusion.5
  (37 shorter events, 1.1 us)
Async XLA Ops:
  7.2 252.3 %copy-start = (bf16[1,1280,640]{2,1,0:T(8,128)(2,1)S(1)}, bf16[1,1280,640]{2,1,0:T(8,128)(2,1)}, u32[]{:S(2)}) copy-start(bf16[1,1280,640]{2,1,0:T(8,128)(2,1)} %param.14) | copy-start | bytes 4915204
  7.2 40.5 %all-gather.5.cloned.1.call-start = ((), (), s32[]{:S(2)}) async-start(), calls=%async_computation.7 | async-start | bytes 4423680 | tf_op jit(solution)/shard_map/all_gather | solution.py:73
  26.0 28.0 %all-to-all-start = ((bf16[8,32,6]{2,0,1:T(8,128)(2,1)}), bf16[8,32,6]{2,0,1:T(8,128)(2,1)S(1)}, u32[]{:S(2)}, u32[]{:S(2)}) async-start(bf16[8,32,6]{2,0,1:T(8,128)(2,1)} %copy.44), calls=%async_computation | async-start | bytes 131072 | tf_op jit(solution)/shard_map/all_to_all | solution.py:80
  53.9 10.1 %copy-start.5 = (f32[2,1280]{1,0:T(2,128)S(1)}, f32[2,1280]{1,0:T(2,128)}, u32[]{:S(2)}) copy-start(f32[2,1280]{1,0:T(2,128)} %param.13) | copy-start | bytes 30724
  53.9 10.2 %copy-start.7 = (s32[128]{0:T(128)S(1)}, s32[128]{0:T(128)}, u32[]{:S(2)}) copy-start(s32[128]{0:T(128)} %param.12) | copy-start | bytes 1540
  54.0 10.2 %copy-start.4 = (bf16[128,1280]{1,0:T(8,128)(2,1)S(1)}, bf16[128,1280]{1,0:T(8,128)(2,1)}, u32[]{:S(2)}) copy-start(bf16[128,1280]{1,0:T(8,128)(2,1)} %param.9) | copy-start | bytes 983044
  54.0 96.8 %all-to-all-start.2 = ((bf16[8,32,6,1280]{3,0,2,1:T(8,128)(2,1)}), bf16[8,32,6,1280]{3,0,2,1:T(8,128)(2,1)}, u32[]{:S(2)}, u32[]{:S(2)}) async-start(bf16[8,32,6,1280]{3,0,2,1:T(8,128)(2,1)} %copy.51), calls=%async_computation.2 | async-start | bytes 7864320 | tf_op jit(solution)/shard_map/all_to_all | solution.py:78
  64.0 36.7 %all-gather.3.cloned.1.call-start = ((), (), s32[]{:S(2)}) async-start(), calls=%async_computation.6 | async-start | bytes 4423680 | tf_op jit(solution)/shard_map/all_gather | solution.py:74
  150.7 96.1 %all-to-all-start.1 = ((bf16[8,32,6,1280]{3,0,2,1:T(8,128)(2,1)}), bf16[8,32,6,1280]{3,0,2,1:T(8,128)(2,1)}, u32[]{:S(2)}, u32[]{:S(2)}) async-start(bf16[8,32,6,1280]{3,0,2,1:T(8,128)(2,1)} %copy.48), calls=%async_computation.1 | async-start | bytes 7864320 | tf_op jit(solution)/shard_map/all_to_all | solution.py:79
  160.4 269.0 %reduce-scatter.2.cloned.1.call-start = ((), (), s32[]{:S(2)}) async-start(), calls=%async_computation.8 | async-start | bytes 4423680 | tf_op jit(solution)/shard_map/reduce_scatter | solution.py:94
  259.4 5.5 %copy-start.2 = (bf16[1536,1280]{1,0:T(8,128)(2,1)S(1)}, bf16[1536,1280]{1,0:T(8,128)(2,1)}, u32[]{:S(2)}) copy-start(bf16[1536,1280]{1,0:T(8,128)(2,1)} %reshape.51) | copy-start | bytes 11796484
  259.4 5.5 %copy-start.6 = (bf16[1,640,1280]{2,1,0:T(8,128)(2,1)S(1)}, bf16[1,640,1280]{2,1,0:T(8,128)(2,1)}, u32[]{:S(2)}) copy-start(bf16[1,640,1280]{2,1,0:T(8,128)(2,1)} %param.15) | copy-start | bytes 4915204
  265.0 5.5 %copy-start.9 = (f32[1536,640]{1,0:T(8,128)}, f32[1536,640]{1,0:T(8,128)S(1)}, u32[]{:S(2)}) copy-start(f32[1536,640]{1,0:T(8,128)S(1)} %fusion.12) | copy-start | bytes 11796484
  383.2 0.7 copy-start.8
  385.3 18.7 %all-to-all-start.4 = ((bf16[8,32,6]{2,0,1:T(8,128)(2,1)}), bf16[8,32,6]{2,0,1:T(8,128)(2,1)S(1)}, u32[]{:S(2)}, u32[]{:S(2)}) async-start(bf16[8,32,6]{2,0,1:T(8,128)(2,1)} %copy.57), calls=%async_computation.5 | async-start | bytes 131072 | tf_op jit(solution)/shard_map/all_to_all | solution.py:89
  391.9 7.7 %copy-start.1 = (bf16[1536,1280]{1,0:T(8,128)(2,1)S(1)}, bf16[1536,1280]{1,0:T(8,128)(2,1)}, u32[]{:S(2)}) copy-start(bf16[1536,1280]{1,0:T(8,128)(2,1)} %reshape.52) | copy-start | bytes 11796484
  392.0 7.7 %copy-start.3 = (bf16[1536,640]{1,0:T(8,128)(2,1)S(1)}, bf16[1536,640]{1,0:T(8,128)(2,1)}, u32[]{:S(2)}) copy-start(bf16[1536,640]{1,0:T(8,128)(2,1)} %get-tuple-element.7) | copy-start | bytes 5898244
Sparse Core Ops, SparseCore 0:
  12.2 35.4 all-gather.4
  67.3 33.4 all-gather.2
  383.4 36.6 reduce-scatter.1
where the time goes:
time: 441 us; the launch traced here: 438 us
  waiting for transfers between devices  164 us (37%)
  blocking collectives  134 us (30%)
  local copies, waits for them, and re-layouts  55.4 us (13%)
  starting transfers between devices  36.9 us (8%)
  matrix products  32.1 us (7%)
  between operations  14 us (3%)
    all_to_all x1, blocking collectives, local(): lax.all_to_all(token_part.astype(jnp.bfloat16), 'expert', split_axis=1, c...  98.1 us
    all_to_all x1, waiting for transfers between devices, local(): lax.all_to_all(col_grad, 'expert', split_axis=1, concat_axis=1, tiled=True)  73.2 us
    all_to_all x1, waiting for transfers between devices, local(): lax.all_to_all(col_in, 'expert', split_axis=1, concat_axis=1, tiled=True)  43.8 us
    all_gather x1, waiting for transfers between devices, local(): lax.all_gather(send_grad[None], 'dp', axis=0, tiled=True)  35.2 us
    unnamed x1, blocking collectives  23.7 us
    all_gather x1, blocking collectives, local(): lax.all_gather(send_gate[None], 'dp', axis=0, tiled=True)  12.1 us
    all_gather x1, waiting for transfers between devices, local(): lax.all_gather(send_in[None], 'dp', axis=0, tiled=True)  11.4 us
    all_to_all x1, starting transfers between devices, local(): lax.all_to_all(col_gate, 'expert', split_axis=1, concat_axis=1, tiled=True)  10.3 us
  transfers between devices with their start and end apart: 7, of which 4 were waited for; matrix products, arithmetic and copies ran while one was open for 10% of the time, Pallas kernels for 0%

commit v1 on v0

v1 whole, which is shorter than its diff:
```python
import jax
import jax.numpy as jnp
from jax import lax
from jax.sharding import PartitionSpec as P

inv_root_two = 0.7071067811865476
inv_root_two_pi = 0.3989422804014327


def gelu_parts(pre_act):
    normal_cdf = 0.5 * (1.0 + lax.erf(pre_act * inv_root_two))
    density = jnp.exp(-0.5 * pre_act * pre_act) * inv_root_two_pi
    return (pre_act * normal_cdf, normal_cdf + pre_act * density)


def local(tokens, grad_out, gate, expert_ids, modality, modal_gain, w_in, w_out):
    experts = lax.axis_size("expert")
    tok_rows, width = tokens.shape
    cap = 3 * tok_rows // (2 * experts)
    chosen = expert_ids[:, 0]
    ids = jnp.arange(tok_rows, dtype=jnp.int32)
    same = (chosen[:, None] == chosen[None, :]) & (ids[None, :] < ids[:, None])
    slot_pos = jnp.sum(same.astype(jnp.int32), axis=1)
    target = chosen * cap + slot_pos
    select = (jnp.arange(experts * cap, dtype=jnp.int32)[:, None] == target[None, :]).astype(jnp.bfloat16)
    gate_wide = gate.astype(jnp.float32)
    gain_rows = jnp.where(modality[:, None] == 1, modal_gain[1][None, :], modal_gain[0][None, :])
    gated = (gate_wide[:, None] * gain_rows * grad_out.astype(jnp.float32)).astype(jnp.bfloat16)
    both = jnp.concatenate([tokens, gated], axis=1)
    send = jnp.dot(select, both, preferred_element_type=jnp.float32).astype(jnp.bfloat16)
    got = lax.all_to_all(send.reshape(experts, cap, 2 * width), "expert", split_axis=0, concat_axis=0, tiled=True)
    rows = lax.all_gather(got.reshape(experts * cap, 2 * width), "dp", axis=0, tiled=True)
    rows_in, rows_grad = rows[:, :width], rows[:, width:]
    weight_in, weight_out = w_in[0], w_out[0]
    pre_act = jnp.dot(rows_in, weight_in, preferred_element_type=jnp.float32)
    activation, slope = gelu_parts(pre_act)
    back_grad = lax.dot_general(rows_grad, weight_out, (((1,), (1,)), ((), ())), preferred_element_type=jnp.float32)
    gate_part = jnp.sum(activation * back_grad, axis=1)
    pre_grad = (back_grad * slope).astype(jnp.bfloat16)
    token_part = lax.dot_general(pre_grad, weight_in, (((1,), (1,)), ((), ())), preferred_element_type=jnp.float32)
    parts = jnp.concatenate(
        [token_part.astype(jnp.bfloat16), jnp.broadcast_to(gate_part.astype(jnp.bfloat16)[:, None], (rows.shape[0], 128))],
        axis=1,
    )
    summed = lax.psum_scatter(parts, "dp", scatter_dimension=0, tiled=True)
    home = lax.all_to_all(
        summed.reshape(experts, cap, width + 128), "expert", split_axis=0, concat_axis=0, tiled=True
    ).reshape(experts * cap, width + 128)
    out_grads = lax.dot_general(
        activation.astype(jnp.bfloat16), rows_grad, (((0,), (0,)), ((), ())), preferred_element_type=jnp.float32
    )
    in_grads = lax.dot_general(rows_in, pre_grad, (((0,), (0,)), ((), ())), preferred_element_type=jnp.float32)
    result = lax.dot_general(select, home, (((0,), (0,)), ((), ())), preferred_element_type=jnp.float32)
    return (
        result[:, :width].astype(jnp.bfloat16),
        (result[:, width] / gate_wide).astype(jnp.bfloat16),
        in_grads.astype(jnp.bfloat16)[None],
        out_grads.astype(jnp.bfloat16)[None],
    )


def solution(mesh):
    rows = P(("dp", "expert"), None)
    flat = P(("dp", "expert"))
    return jax.shard_map(
        local,
        mesh=mesh,
        in_specs=(rows, rows, flat, rows, flat, P(), P("expert", None, "dp"), P("expert", "dp", None)),
        out_specs=(rows, flat, P("expert", None, "dp"), P("expert", "dp", None)),
        check_vma=False,
    )
```

time: 441 us -> 216 us (0.49)
  blocking collectives: 134 us -> 43.3 us
  waiting for transfers between devices: 164 us -> 92.7 us
  local copies, waits for them, and re-layouts: 55.4 us -> 14.1 us
  starting transfers between devices: 36.9 us -> 9.98 us
    all_to_all x4 -> x1, waiting for transfers between devices: 117 us -> 3.62 us  [local(): lax.all_to_all(summed.reshape(experts, cap, width + 128), 'expert', split...]
    all_to_all x1, blocking collectives: 98.1 us -> 43.3 us  [local(): lax.all_to_all(send.reshape(experts, cap, 2 * width), 'expert', split_axi...]
    reduce_scatter x1, waiting for transfers between devices: 0.01 us -> 41.1 us  [local(): summed = lax.psum_scatter(parts, 'dp', scatter_dimension=0, tiled=True)]
    all_to_all x4 -> x1, starting transfers between devices: 36.6 us -> 9.9 us  [local(): lax.all_to_all(summed.reshape(experts, cap, width + 128), 'expert', split...]
    unnamed x1 -> x0, blocking collectives: 23.7 us -> none
    all_to_all x5 -> x0, local copies, waits for them, and re-layouts: 14.1 us -> none  [the longest x1 5.38 us: local(): lax.all_to_all(col_in, 'expert', split_axis=1, concat_axis=1, tiled=True)]
    all_gather x3 -> x0, local copies, waits for them, and re-layouts: 13.2 us -> none  [the longest x1 6.24 us: local(): lax.all_gather(send_in[None], 'dp', axis=0, tiled=True)]
    all_gather x1 -> x0, blocking collectives: 12.1 us -> none  [local(): lax.all_gather(send_gate[None], 'dp', axis=0, tiled=True)]
  transfers between devices with their start and end apart: 7 -> 3, of which waited for: 4 -> 3; matrix products, arithmetic and copies ran while one was open for 10% -> 6% of each run, Pallas kernels for 0% -> 0%
where the time goes in v1:
time: 216 us; the launch traced here: 213 us
  waiting for transfers between devices  92.7 us (43%)
  blocking collectives  43.3 us (20%)
  matrix products  31.9 us (15%)
  between operations  14.2 us (7%)
  local copies, waits for them, and re-layouts  14.1 us (7%)
  starting transfers between devices  9.98 us (5%)
  other arithmetic  6.93 us (3%)
    all_gather x1, waiting for transfers between devices, local(): lax.all_gather(got.reshape(experts * cap, 2 * width), 'dp', axis=0, tiled...  47.9 us
    all_to_all x1, blocking collectives, local(): lax.all_to_all(send.reshape(experts, cap, 2 * width), 'expert', split_axi...  43.3 us
    reduce_scatter x1, waiting for transfers between devices, local(): summed = lax.psum_scatter(parts, 'dp', scatter_dimension=0, tiled=True)  41.1 us
    all_to_all x1, starting transfers between devices, local(): lax.all_to_all(summed.reshape(experts, cap, width + 128), 'expert', split...  9.9 us
    dot_general x1, matrix products, local(): lax.dot_general(rows_in, pre_grad, (((0,), (0,)), ((), ())), preferred_el...  7.31 us
    dot_general x1, matrix products, local(): lax.dot_general(rows_grad, weight_out, (((1,), (1,)), ((), ())), preferre...  7.16 us
    unnamed x13, local copies, waits for them, and re-layouts  6.45 us
    dot_general x1, matrix products, local(): lax.dot_general(activation.astype(jnp.bfloat16), rows_grad, (((0,), (0,))...  6.23 us
  transfers between devices with their start and end apart: 3, of which 3 were waited for; matrix products, arithmetic and copies ran while one was open for 6% of the time, Pallas kernels for 0%

profile of v1, /device:TPU:96, one launch (start us, length us, event | category | flops | bytes accessed | tf_op | source)
XLA Modules:
  0.0 213.1 jit_solution(11620323519230938463)
XLA Ops:
  7.2 0.0 copy-start
  7.2 0.0 all-gather.2.cloned.1.call-start
  7.2 0.8 broadcast_compare_fusion
  8.0 0.9 convert_reduce_fusion
  8.9 0.7 multiply_add_fusion
  9.6 0.7 convert_element_type.43
  10.2 0.8 slice_reduce_fusion.2
  11.0 1.2 multiply_convert_fusion
  12.2 2.3 %convolution_convert_fusion.1 = bf16[192,2560]{1,0:T(8,128)(2,1)} fusion(bf16[128,1280]{1,0:T(8,128)(2,1)S(1)} %multiply_convert_fusion, bf16[128,1280]{1,0:T(8,128)(2,1)} %param.8, s32[128]{0:T(128)S(1)} %multiply_add_fusion), kind=kOutput, calls=%fused_computation.11 | convolution fusion | flops 127655936 | bytes 1638912 | tf_op jit(solution)/shard_map/dot_general | solution.py:30
  14.5 1.4 reshape.35
  15.9 43.3 %all_to_all.10 = bf16[32,6,2560]{2,1,0:T(8,128)(2,1)} all-to-all(bf16[32,6,2560]{2,1,0:T(8,128)(2,1)S(1)} %reshape.35), channel_id=1, replica_groups=mesh['dp'=8,'expert'=32] {'expert'}, dimensions={0} | all-to-all | bytes 1966080 | tf_op jit(solution)/shard_map/all_to_all | solution.py:31
  59.2 2.2 %reshape.36 = bf16[192,2560]{1,0:T(8,128)(2,1)} reshape(bf16[32,6,2560]{2,1,0:T(8,128)(2,1)} %all_to_all.10) | data formatting | bytes 1966080 | tf_op jit(solution)/shard_map/reshape | solution.py:32
  61.4 0.0 all-gather.2.cloned.1.call-update
  61.5 0.0 reduce-scatter.4.cloned.1.call-start
  61.5 47.9 %all-gather.2.cloned.1.call-done = bf16[1536,2560]{1,0:T(8,128)(2,1)} async-done(((bf16[192,2560]{1,0:T(8,128)(2,1)}), bf16[1536,2560]{1,0:T(8,128)(2,1)}) %all-gather.2.cloned.1.call-update) | async-done | bytes 7864336 | tf_op jit(solution)/shard_map/all_gather | solution.py:32
  109.5 0.0 copy-done
  109.5 0.0 copy-start.1
  109.5 5.1 %fusion.8 = f32[1536,640]{0,1:T(8,128)S(1)} fusion(bf16[1536,2560]{1,0:T(8,128)(2,1)} %all-gather.2.cloned.1.call-done, bf16[1,1280,640]{2,1,0:T(8,128)(2,1)S(1)} %copy-done), kind=kOutput, calls=%fused_computation.14 | convolution fusion | flops 2516582400 | bytes 9502720 | tf_op jit(solution)/shard_map/dot_general | solution.py:35
  114.6 0.0 copy-done.1
  114.6 0.0 copy-start.3
  114.6 7.2 %fusion.5 = (bf16[1536,640]{0,1:T(8,128)(2,1)S(1)}, bf16[1536]{0:T(1024)(128)(2,1)S(1)}) fusion(f32[1536,640]{0,1:T(8,128)S(1)} %fusion.8, bf16[1,640,1280]{2,1,0:T(8,128)(2,1)} %param.15, bf16[1536,2560]{1,0:T(8,128)(2,1)S(1)} %copy-done.1), kind=kOutput, calls=%fused_computation.8 | convolution fusion | flops 2529360384 | bytes 11471872 | tf_op jit(solution)/shard_map/dot_general | solution.py:37
  121.8 0.0 copy-done.3
  121.8 0.0 copy-start.5
  121.8 3.5 %convolution_convert_fusion = bf16[1536,1280]{0,1:T(8,128)(2,1)S(1)} fusion(bf16[1536,640]{0,1:T(8,128)(2,1)S(1)} %get-tuple-element.6, bf16[1,1280,640]{2,1,0:T(8,128)(2,1)S(1)} %copy-done), kind=kOutput, calls=%fused_computation | convolution fusion | flops 2518548480 | bytes 7536640 | tf_op jit(solution)/shard_map/dot_general | solution.py:40
  125.3 0.0 copy-done.5
  125.3 2.3 %pad_maximum_fusion = bf16[1536,1408]{0,1:T(8,128)(2,1)} fusion(bf16[1536,128]{0,1:T(8,128)(2,1)S(1)} %broadcast_in_dim.51, bf16[1536,1280]{0,1:T(8,128)(2,1)S(1)} %convolution_convert_fusion), kind=kLoop, calls=%fused_computation.2 | loop fusion | flops 8650752 | bytes 8650752 | tf_op jit(solution)/shard_map/concatenate | solution.py:41
  127.6 6.4 %copy.15 = bf16[1536,1408]{1,0:T(8,128)(2,1)} copy(bf16[1536,1408]{0,1:T(8,128)(2,1)} %pad_maximum_fusion) | data formatting | bytes 8650752
  134.0 0.0 reduce-scatter.4.cloned.1.call-update
  134.0 41.1 %reduce-scatter.4.cloned.1.call-done = bf16[192,1408]{1,0:T(8,128)(2,1)} async-done(((bf16[1536,1408]{1,0:T(8,128)(2,1)}), bf16[192,1408]{1,0:T(8,128)(2,1)}) %reduce-scatter.4.cloned.1.call-update) | async-done | bytes 540688 | tf_op jit(solution)/shard_map/reduce_scatter | solution.py:45
  175.1 2.1 reshape.37
  177.2 9.9 %all-to-all-start.1 = ((bf16[32,6,1408]{2,1,0:T(8,128)(2,1)}), bf16[32,6,1408]{2,1,0:T(8,128)(2,1)S(1)}, u32[]{:S(2)}, u32[]{:S(2)}) async-start(bf16[32,6,1408]{2,1,0:T(8,128)(2,1)} %reshape.37), calls=%async_computation.1 | async-start | bytes 1441792 | tf_op jit(solution)/shard_map/all_to_all | solution.py:46
  187.2 0.0 copy-start.4
  187.2 7.3 %fusion.20 = bf16[1,1280,640]{2,1,0:T(8,128)(2,1)} fusion(bf16[1536,640]{0,1:T(8,128)(2,1)} %copy-done.5, bf16[1536,2560]{1,0:T(8,128)(2,1)} %all-gather.2.cloned.1.call-done), kind=kOutput, calls=%fused_computation.22 | convolution fusion | flops 2517401600 | bytes 7536640 | tf_op jit(solution)/shard_map/dot_general | solution.py:52
  194.5 0.0 copy-done.4
  194.5 0.0 copy-start.2
  194.5 6.2 %fusion.23 = bf16[1,640,1280]{2,1,0:T(8,128)(2,1)} fusion(bf16[1536,2560]{1,0:T(8,128)(2,1)} %all-gather.2.cloned.1.call-done, f32[1536,640]{0,1:T(8,128)S(1)} %copy-done.4), kind=kOutput, calls=%fused_computation.23 | convolution fusion | flops 2522316800 | bytes 9502720 | tf_op jit(solution)/shard_map/dot_general | solution.py:49
  200.7 3.6 %all-to-all-done.1 = bf16[32,6,1408]{2,1,0:T(8,128)(2,1)S(1)} async-done(((bf16[32,6,1408]{2,1,0:T(8,128)(2,1)}), bf16[32,6,1408]{2,1,0:T(8,128)(2,1)S(1)}, u32[]{:S(2)}, u32[]{:S(2)}) %all-to-all-start.1) | async-done | bytes 540704 | tf_op jit(solution)/shard_map/all_to_all | solution.py:46
  204.3 0.2 reshape.38
  204.5 0.3 fusion.34
  204.8 0.1 slice_reduce_fusion
  204.9 0.8 slice.49
  205.7 0.0 copy-done.2
  205.7 0.5 divide_convert_fusion
  (1 shorter events, 0.0 us)
Async XLA Ops:
  7.2 102.3 %copy-start = (bf16[1,1280,640]{2,1,0:T(8,128)(2,1)S(1)}, bf16[1,1280,640]{2,1,0:T(8,128)(2,1)}, u32[]{:S(2)}) copy-start(bf16[1,1280,640]{2,1,0:T(8,128)(2,1)} %param.14) | copy-start | bytes 4915204
  7.2 102.3 %all-gather.2.cloned.1.call-start = ((), (), s32[]{:S(2)}) async-start(), calls=%async_computation.3 | async-start | bytes 8847360 | tf_op jit(solution)/shard_map/all_gather | solution.py:32
  61.5 113.7 %reduce-scatter.4.cloned.1.call-start = ((), (), s32[]{:S(2)}) async-start(), calls=%async_computation.4 | async-start | bytes 4866048 | tf_op jit(solution)/shard_map/reduce_scatter | solution.py:45
  109.5 5.2 %copy-start.1 = (bf16[1536,2560]{1,0:T(8,128)(2,1)S(1)}, bf16[1536,2560]{1,0:T(8,128)(2,1)}, u32[]{:S(2)}) copy-start(bf16[1536,2560]{1,0:T(8,128)(2,1)} %all-gather.2.cloned.1.call-done) | copy-start | bytes 23592964
  114.6 7.2 %copy-start.3 = (f32[1536,640]{0,1:T(8,128)}, f32[1536,640]{0,1:T(8,128)S(1)}, u32[]{:S(2)}) copy-start(f32[1536,640]{0,1:T(8,128)S(1)} %fusion.8) | copy-start | bytes 11796484
  121.8 3.5 %copy-start.5 = (bf16[1536,640]{0,1:T(8,128)(2,1)}, bf16[1536,640]{0,1:T(8,128)(2,1)S(1)}, u32[]{:S(2)}) copy-start(bf16[1536,640]{0,1:T(8,128)(2,1)S(1)} %get-tuple-element.6) | copy-start | bytes 5898244
  177.2 27.1 %all-to-all-start.1 = ((bf16[32,6,1408]{2,1,0:T(8,128)(2,1)}), bf16[32,6,1408]{2,1,0:T(8,128)(2,1)S(1)}, u32[]{:S(2)}, u32[]{:S(2)}) async-start(bf16[32,6,1408]{2,1,0:T(8,128)(2,1)} %reshape.37), calls=%async_computation.1 | async-start | bytes 1441792 | tf_op jit(solution)/shard_map/all_to_all | solution.py:46
  187.2 7.3 %copy-start.4 = (f32[1536,640]{0,1:T(8,128)S(1)}, f32[1536,640]{0,1:T(8,128)}, u32[]{:S(2)}) copy-start(f32[1536,640]{0,1:T(8,128)} %copy-done.3) | copy-start | bytes 11796484
  194.5 11.2 %copy-start.2 = (bf16[128]{0:T(256)(128)(2,1)S(1)}, bf16[128]{0:T(256)(128)(2,1)}, u32[]{:S(2)}) copy-start(bf16[128]{0:T(256)(128)(2,1)} %param.10) | copy-start | bytes 772
Sparse Core Ops, SparseCore 0:
  61.6 47.8 all-gather.1
  134.2 40.9 reduce-scatter.3

commit v2 on v1

v2 whole, which is shorter than its diff:
```python
import functools

import jax
import jax.numpy as jnp
from jax import lax
from jax.experimental import pallas as pl
from jax.experimental.pallas import tpu as pltpu
from jax.sharding import PartitionSpec as P

MESH = pl.DeviceIdType.MESH
BF = jnp.bfloat16
F32 = jnp.float32
I32 = jnp.int32
ROOT = 0.7071067811865476
ROOT_PI = 0.3989422804014327

T, D, F, CAP = 128, 1280, 640, 6
NZ, NX, NY = 8, 4, 4
Q, GS = 4, 8
RG = GS * CAP
M = 8 * RG
FW, BW = 1024, 512
PW = 3 * D + 128
CUT = 2048


def iota(shape, dim):
    return lax.broadcasted_iota(I32, shape, dim)


def onehot(cond):
    return jnp.where(cond, 1.0, 0.0).astype(BF)


def mm(a, b):
    return jnp.dot(a, b, preferred_element_type=F32)


def mm_nt(a, b):
    return lax.dot_general(a, b, (((1,), (1,)), ((), ())), preferred_element_type=F32)


def mm_tn(a, b):
    return lax.dot_general(a, b, (((0,), (0,)), ((), ())), preferred_element_type=F32)


def sixth(v):
    return ((v.astype(F32) + 0.5) * (1.0 / 6.0)).astype(I32)


def offset(k):
    pair = k // NX
    far = (pair + 1) // 2
    return far * (2 * (pair % 2) - 1), k % NX


def kernel(tok_ref, grad_ref, gate_ref, ids_ref, mod_ref, gain_ref, win_hbm, wout_hbm,
           gtok_ref, ggate_ref, gwin_hbm, gwout_hbm,
           out_buf, in_buf, rows, win, wout, pre, back, act16, pre16, part, sib, far, near, ret, home,
           acc_in, acc_out, st_in, st_out, tgt_s,
           w_sem, o_sem, as_sem, ar_sem, gs_sem, gr_sem, rs_sem, rr_sem, bs_sem, br_sem):
    dp, ex = lax.axis_index("dp"), lax.axis_index("expert")
    y, c = dp // 2, dp % 2
    z, x = ex // NX, ex % NX

    def column(step, core):
        return ((y + step + NY) % NY) * 2 + core

    up, down, other = {"dp": column(1, c)}, {"dp": column(-1, c)}, {"dp": y * 2 + 1 - c}

    def target(k):
        dz, dx = offset(k)
        return {"expert": ((z - dz + NZ) % NZ) * NX + (x - dx + NX) % NX}

    def source(k):
        dz, dx = offset(k)
        return {"expert": ((z + dz + NZ) % NZ) * NX + (x + dx) % NX}

    barrier = pltpu.get_barrier_semaphore()

    @pl.loop(1, NZ * NX)
    def _(k):
        pl.semaphore_signal(barrier, inc=1, device_id=target(k), device_id_type=MESH)

    for peer in (up, down, other):
        pl.semaphore_signal(barrier, inc=1, device_id=peer, device_id_type=MESH)

    load_in = pltpu.make_async_copy(win_hbm, win, w_sem.at[0])
    load_out = pltpu.make_async_copy(wout_hbm, wout, w_sem.at[1])
    load_in.start()
    load_out.start()

    def rdma(src, dst, ssem, rsem, dev):
        return pltpu.make_async_remote_copy(
            src_ref=src, dst_ref=dst, send_sem=ssem, recv_sem=rsem, device_id=dev, device_id_type=MESH
        )

    ids = ids_ref[...]
    wide = jnp.broadcast_to(ids.astype(F32), (T, T))
    same = (wide == wide.T) & (iota((T, T), 0) < iota((T, T), 1))
    slot = jnp.sum(jnp.where(same, 1.0, 0.0), axis=0, keepdims=True).astype(I32)
    tz, tx = ids >> 2, ids & 3
    dz = (z - tz + NZ) & (NZ - 1)
    pair = jnp.where(dz == 0, 0, jnp.where(dz <= NZ // 2, 2 * dz - 1, 2 * (NZ - dz)))
    first = (pair * NX + ((x - tx + NX) & (NX - 1))) * 16

    gate_col = jnp.broadcast_to(gate_ref[...].astype(F32), (T, T)).T[:, 0:1]
    mod_col = jnp.broadcast_to(mod_ref[...].astype(F32), (T, T)).T[:, 0:1]
    gain = jnp.where(mod_col == 1.0, gain_ref[1:2, :], gain_ref[0:1, :])
    tok = tok_ref[...]
    gated = (gate_col * gain * grad_ref[...].astype(F32)).astype(BF)

    def tail(piece, j):
        return jnp.where((piece & 3) == j, first + 12 + (piece >> 2), -1)

    where_rows = [first + slot, first + 6 + slot]
    where_tail = [[tail(slot, j), tail(slot + 6, j)] for j in range(4)]

    def pack(q):
        lines = iota((GS * 16, T), 0) + q * GS * 16
        body = [onehot(lines == w) for w in where_rows]
        for j in range(4):
            lhs = jnp.concatenate(body + [onehot(lines == w) for w in where_tail[j]], axis=1)
            cols = slice(256 * j, 256 * j + 256)
            rhs = jnp.concatenate([tok[:, cols], gated[:, cols], tok[:, FW:], gated[:, FW:]], axis=0)
            out_buf[q * GS:(q + 1) * GS, :, cols] = mm(lhs, rhs).astype(BF).reshape(GS, 16, 256)

    def a2a(k):
        return rdma(out_buf.at[k], in_buf.at[k], as_sem.at[k], ar_sem.at[k], target(k))

    for q in range(Q):
        pack(q)
        if q == 0:
            in_buf[0] = out_buf[0]
            pl.semaphore_wait(barrier, NZ * NX - 1 + 3)

        @pl.loop(max(1, q * GS), (q + 1) * GS)
        def _(k):
            a2a(k).start()

    cc = iota((1, GS * 16), 1)
    cs, ci = cc >> 4, cc & 15
    row_body = jnp.where(ci < 6, cs * 6 + ci, jnp.where(ci < 12, RG + cs * 6 + ci - 6, -1))

    def row_tail(j):
        p = (ci - 12) * 4 + j
        return jnp.where((ci >= 12) & (ci < 15), jnp.where(p < 6, cs * 6 + p, RG + cs * 6 + p - 6), -1)

    lines96 = iota((2 * RG, GS * 16), 0)
    un_body = onehot(lines96 == row_body)
    un_tail = jnp.concatenate([onehot(lines96 == row_tail(j)) for j in range(4)], axis=1)

    def gather(q, role):
        mine, below, above = dp, column(-1, c), column(1, c)
        beyond = column(2, c)
        d, half, dev = [
            (mine, None, up), (mine, None, down), (below, 0, up), (above, 1, down),
            (mine, None, other), (below, None, other), (above, None, other), (beyond, 0, other), (beyond, 1, other),
        ][role]
        ref = rows.at[q, d] if half is None else rows.at[q, d, half]
        return rdma(ref, ref, gs_sem.at[q, role], gr_sem.at[q, role], dev)

    def gather_wait(q, role):
        half = {2: 0, 3: 1, 7: 0, 8: 1}.get(role)
        d = {0: column(-1, c), 1: column(1, c), 2: column(2, c), 3: column(2, c), 4: column(0, 1 - c),
             5: column(-1, 1 - c), 6: column(1, 1 - c), 7: column(2, 1 - c), 8: column(2, 1 - c)}[role]
        ref = rows.at[q, d] if half is None else rows.at[q, d, half]
        rdma(ref, ref, gs_sem.at[q, role], gr_sem.at[q, role], other).wait_recv()

    def first_step(q):
        @pl.loop(max(1, q * GS), (q + 1) * GS)
        def _(k):
            a2a(k).wait_recv()

        got = in_buf[q * GS:(q + 1) * GS].reshape(GS * 16, FW)
        main = mm(un_body, got).astype(BF)
        stack = jnp.concatenate([got[:, 256 * j:256 * j + 256] for j in range(4)], axis=0)
        rest = mm(un_tail, stack).astype(BF)
        for h in range(2):
            rows[q, dp, h, :, 0:FW] = main[h * RG:(h + 1) * RG]
            rows[q, dp, h, :, FW:D] = rest[h * RG:(h + 1) * RG]
        for role in (0, 1, 4):
            gather(q, role).start()

    def second_step(q):
        gather_wait(q, 0)
        gather(q, 2).start()
        gather(q, 5).start()
        gather_wait(q, 1)
        gather(q, 3).start()
        gather(q, 6).start()

    def third_step(q):
        gather_wait(q, 2)
        gather(q, 7).start()
        gather_wait(q, 3)
        gather(q, 8).start()

    lane6 = iota((M, 128), 1)
    row_m = iota((M, 128), 0)
    gate_spread = lane6 == row_m - 6 * sixth(row_m)
    rr = iota((T, M), 0)
    gate_pick = onehot(((rr & 15) < 8) & (sixth(iota((T, M), 1)) == (rr >> 4) * 8 + (rr & 15)))

    def compute(q):
        for role in range(4, 9):
            gather_wait(q, role)
        pre[...] = mm(rows[q, :, 0].reshape(M, D), win[...])
        back[...] = mm_nt(rows[q, :, 1].reshape(M, D), wout[...])
        gates = []
        for r in range(0, M, 128):
            u = pre[r:r + 128]
            b = back[r:r + 128]
            cdf = 0.5 * (1.0 + lax.erf(u * ROOT))
            density = jnp.exp(-0.5 * u * u) * ROOT_PI
            act = u * cdf
            act16[q, r:r + 128] = act.astype(BF)
            pre16[q, r:r + 128] = (b * (cdf + u * density)).astype(BF)
            gates.append(jnp.sum(act * b, axis=1, keepdims=True))
        gate_sum = jnp.concatenate(gates, axis=0)
        spread = jnp.where(gate_spread, gate_sum, 0.0).astype(BF)
        part[q, :, :, 3 * D:PW] = mm(gate_pick, spread).astype(BF).reshape(8, 16, 128)
        tokens = mm_nt(pre16[q], win[...]).astype(BF).reshape(8, 3, 16, D)
        for g in range(3):
            part[q, :, :, g * D:(g + 1) * D] = tokens[:, g]
        for j in range(NY):
            pair_sum(q, j).start()

    def pair_sum(q, j):
        return rdma(part.at[q, column(j, 1 - c)], sib.at[q, j], rs_sem.at[q, j], rr_sem.at[q, j], other)

    def ring(q, role):
        src, dst, dev = [
            (part.at[q, column(2, c), :, 0:CUT], far.at[q, 0, :, 0:CUT], up),
            (part.at[q, column(2, c), :, CUT:PW], far.at[q, 1, :, 0:PW - CUT], down),
            (part.at[q, column(1, c)], near.at[q, 0], up),
            (part.at[q, column(-1, c)], near.at[q, 1], down),
        ][role]
        return rdma(src, dst, rs_sem.at[q, 4 + role], rr_sem.at[q, 4 + role], dev)

    def add_pair(q, j):
        pair_sum(q, j).wait_recv()
        d = column(j, c)
        part[q, d] = (part[q, d].astype(F32) + sib[q, j].astype(F32)).astype(BF)

    def reduce_far(q):
        add_pair(q, 2)
        ring(q, 0).start()
        ring(q, 1).start()

    def reduce_near(q):
        add_pair(q, 1)
        ring(q, 0).wait_recv()
        d = column(1, c)
        part[q, d, :, 0:CUT] = (part[q, d, :, 0:CUT].astype(F32) + far[q, 0].astype(F32)).astype(BF)
        ring(q, 2).start()
        add_pair(q, 3)
        ring(q, 1).wait_recv()
        d = column(-1, c)
        part[q, d, :, CUT:PW] = (part[q, d, :, CUT:PW].astype(F32) + far[q, 1, :, 0:PW - CUT].astype(F32)).astype(BF)
        ring(q, 3).start()

    br = iota((GS * 16, 3 * RG), 0)
    bs, bi = br >> 4, br & 15
    bc = iota((GS * 16, 3 * RG), 1)

    def back_pick(h):
        return onehot(bc == jnp.where(bi < 6, bs * 6 + bi, jnp.where(
            bi < 12, RG + bs * 6 + bi - 6, jnp.where(bi < 15, 2 * RG + bs * 6 + bi - 12 + 3 * h, -1))))

    back_picks = [back_pick(0), back_pick(1)]
    gr = iota((GS * 16, 16), 0)
    gate_line = onehot(((gr & 15) == 15) & (iota((GS * 16, 16), 1) == (gr >> 4)))

    def give_back(k):
        return rdma(ret.at[k], home.at[k], bs_sem.at[k], br_sem.at[k], source(k))

    def reduce_own(q):
        pair_sum(q, 0).wait_recv()
        total = part[q, dp].astype(F32) + sib[q, 0].astype(F32)
        ring(q, 2).wait_recv()
        ring(q, 3).wait_recv()
        total = (total + near[q, 0].astype(F32) + near[q, 1].astype(F32)).astype(BF)
        flat = jnp.concatenate([total[:, g * D:(g + 1) * D] for g in range(3)], axis=0)
        gates = mm(gate_line, total[:, 3 * D:PW])
        for h in range(2):
            rhs = jnp.concatenate(
                [flat[:, 256 * h:256 * h + 256], flat[:, 512 + 256 * h:768 + 256 * h], flat[:, 1024:1280]], axis=0
            )
            res = mm(back_picks[h], rhs)
            if h == 0:
                res = jnp.concatenate([res[:, 0:128] + gates, res[:, 128:256]], axis=1)
            ret[q * GS:(q + 1) * GS, :, 256 * h:256 * h + 256] = res.astype(BF).reshape(GS, 16, 256)
        if q == 0:
            home[0] = ret[0]

        @pl.loop(max(1, q * GS), (q + 1) * GS)
        def _(k):
            give_back(k).start()

    def weight_grads(half):
        q0 = 2 * half
        a = act16[q0:q0 + 2].reshape(2 * M, F)
        p = pre16[q0:q0 + 2].reshape(2 * M, F)
        g_all = rows[q0:q0 + 2, :, 1].reshape(2 * M, D)
        x_all = rows[q0:q0 + 2, :, 0].reshape(2 * M, D)
        go = mm_tn(a, g_all)
        gi = mm_tn(x_all, p)
        if half == 0:
            acc_out[...] = go
            acc_in[...] = gi
        else:
            st_out[...] = (acc_out[...] + go).astype(BF)
            st_in[...] = (acc_in[...] + gi).astype(BF)

    first_step(0)
    second_step(0)
    first_step(1)
    third_step(0)
    load_in.wait()
    load_out.wait()
    second_step(1)
    compute(0)
    first_step(2)
    third_step(1)
    reduce_far(0)
    second_step(2)
    reduce_near(0)
    compute(1)
    first_step(3)
    third_step(2)
    reduce_far(1)
    reduce_own(0)
    second_step(3)
    reduce_near(1)
    compute(2)
    third_step(3)
    reduce_far(2)
    reduce_own(1)
    weight_grads(0)
    reduce_near(2)
    compute(3)
    reduce_far(3)
    reduce_own(2)
    reduce_near(3)
    weight_grads(1)
    store_in = pltpu.make_async_copy(st_in, gwin_hbm, o_sem.at[0])
    store_out = pltpu.make_async_copy(st_out, gwout_hbm, o_sem.at[1])
    store_in.start()
    store_out.start()
    reduce_own(3)

    @pl.loop(1, NZ * NX)
    def _(k):
        give_back(k).wait_recv()

    tgt_s[...] = jnp.broadcast_to(first.astype(F32), (T, T)).T
    first_col = tgt_s[:, 0:1].astype(I32)
    slot_col = jnp.broadcast_to(slot.astype(F32), (T, T)).T[:, 0:1].astype(I32)
    lanes = iota((T, NZ * NX * 16), 1)
    back_rows = home[...].reshape(NZ * NX * 16, BW)
    gtok_ref[:, 0:512] = mm(onehot(lanes == first_col + slot_col), back_rows).astype(BF)
    gtok_ref[:, 512:1024] = mm(onehot(lanes == first_col + 6 + slot_col), back_rows).astype(BF)
    low = jnp.where(slot_col < 3, first_col + 12 + slot_col, -1)
    high = jnp.where(slot_col < 3, -1, first_col + 9 + slot_col)
    gtok_ref[:, 1024:1280] = (
        mm(onehot(lanes == low), back_rows[:, 0:256]) + mm(onehot(lanes == high), back_rows[:, 256:512])
    ).astype(BF)
    gate_lines = mm(onehot(lanes == first_col + 15), back_rows[:, 0:128])
    gate_tok = jnp.sum(jnp.where(iota((T, 128), 1) == slot_col, gate_lines, 0.0), axis=1, keepdims=True) / gate_col
    ggate_ref[...] = jnp.broadcast_to(gate_tok, (T, T)).T[0:1, :].astype(BF)

    @pl.loop(1, NZ * NX)
    def _(k):
        a2a(k).wait_send()
        give_back(k).wait_send()

    for q in range(Q):
        for role in range(9):
            gather(q, role).wait_send()
        for j in range(NY):
            pair_sum(q, j).wait_send()
        for role in range(4):
            ring(q, role).wait_send()
    store_in.wait()
    store_out.wait()


def local(tokens, grad_out, gate, expert_ids, modality, modal_gain, w_in, w_out):
    vmem = pl.BlockSpec(memory_space=pltpu.VMEM)
    hbm = pl.BlockSpec(memory_space=pl.ANY)
    dma = pltpu.SemaphoreType.DMA
    grad_tokens, grad_gate, grad_in, grad_out_w = pl.pallas_call(
        kernel,
        out_shape=[
            jax.ShapeDtypeStruct((T, D), BF),
            jax.ShapeDtypeStruct((1, T), BF),
            jax.ShapeDtypeStruct((D, F), BF),
            jax.ShapeDtypeStruct((F, D), BF),
        ],
        in_specs=[vmem] * 6 + [hbm] * 2,
        out_specs=[vmem, vmem, hbm, hbm],
        scratch_shapes=[
            pltpu.VMEM((NZ * NX, 16, FW), BF),
            pltpu.VMEM((NZ * NX, 16, FW), BF),
            pltpu.VMEM((Q, 8, 2, RG, D), BF),
            pltpu.VMEM((D, F), BF),
            pltpu.VMEM((F, D), BF),
            pltpu.VMEM((M, F), F32),
            pltpu.VMEM((M, F), F32),
            pltpu.VMEM((Q, M, F), BF),
            pltpu.VMEM((Q, M, F), BF),
            pltpu.VMEM((Q, 8, 16, PW), BF),
            pltpu.VMEM((Q, NY, 16, PW), BF),
            pltpu.VMEM((Q, 2, 16, CUT), BF),
            pltpu.VMEM((Q, 2, 16, PW), BF),
            pltpu.VMEM((NZ * NX, 16, BW), BF),
            pltpu.VMEM((NZ * NX, 16, BW), BF),
            pltpu.VMEM((D, F), F32),
            pltpu.VMEM((F, D), F32),
            pltpu.VMEM((D, F), BF),
            pltpu.VMEM((F, D), BF),
            pltpu.VMEM((T, T), F32),
            dma((2,)),
            dma((2,)),
            dma((NZ * NX,)),
            dma((NZ * NX,)),
            dma((Q, 9)),
            dma((Q, 9)),
            dma((Q, 8)),
            dma((Q, 8)),
            dma((NZ * NX,)),
            dma((NZ * NX,)),
        ],
        compiler_params=pltpu.CompilerParams(
            collective_id=0, has_side_effects=True, vmem_limit_bytes=56 * 1024 * 1024
        ),
        cost_estimate=pl.CostEstimate(flops=12_600_000_000, bytes_accessed=8_000_000, transcendentals=2_000_000),
    )(
        tokens,
        grad_out,
        gate.reshape(1, T),
        expert_ids.reshape(1, T),
        modality.reshape(1, T),
        modal_gain,
        w_in[0],
        w_out[0],
    )
    return grad_tokens, grad_gate.reshape(T), grad_in[None], grad_out_w[None]


def solution(mesh):
    rows = P(("dp", "expert"), None)
    flat = P(("dp", "expert"))
    return jax.shard_map(
        local,
        mesh=mesh,
        in_specs=(rows, rows, flat, rows, flat, P(), P("expert", None, "dp"), P("expert", "dp", None)),
        out_specs=(rows, flat, P("expert", None, "dp"), P("expert", "dp", None)),
        check_vma=False,
    )
```

time: 216 us -> 105 us (0.49); the launches traced: 213 us -> 105 us
  Pallas kernels: 0 us -> 97.2 us
  waiting for transfers between devices: 92.7 us -> 0 us
  blocking collectives: 43.3 us -> 0 us
  matrix products: 31.9 us -> 0 us
  between operations: 14.2 us -> 0.64 us
  starting transfers between devices: 9.98 us -> 0 us
  local copies, waits for them, and re-layouts: 14.1 us -> 6.86 us
  other arithmetic: 6.93 us -> 0 us
    pallas_call x0 -> x1, Pallas kernels: none -> 97.2 us  [local(): pl.pallas_call(kernel, out_shape=[jax.ShapeDtypeStruct((T, D), BF), jax.S...]
    all_gather x1 -> x0, waiting for transfers between devices: 47.9 us -> none  [local(): lax.all_gather(got.reshape(experts * cap, 2 * width), 'dp', axis=0, tiled...]
    all_to_all x1 -> x0, blocking collectives: 43.3 us -> none  [local(): lax.all_to_all(send.reshape(experts, cap, 2 * width), 'expert', split_axi...]
    reduce_scatter x1 -> x0, waiting for transfers between devices: 41.1 us -> none  [local(): summed = lax.psum_scatter(parts, 'dp', scatter_dimension=0, tiled=True)]
    dot_general x7 -> x0, matrix products: 31.9 us -> none  [the longest x1 7.31 us: local(): lax.dot_general(rows_in, pre_grad, (((0,), (0,)), ((), ())), preferred_el...]
    all_to_all x1 -> x0, starting transfers between devices: 9.9 us -> none  [local(): lax.all_to_all(summed.reshape(experts, cap, width + 128), 'expert', split...]
    reshape x4 -> x0, local copies, waits for them, and re-layouts: 5.9 us -> none  [the longest x1 2.23 us: local(): got.reshape(experts * cap, 2 * width)]
    all_to_all x1 -> x0, waiting for transfers between devices: 3.62 us -> none  [local(): lax.all_to_all(summed.reshape(experts, cap, width + 128), 'expert', split...]
  transfers between devices with their start and end apart: 3 -> 0, of which waited for: 3 -> 0; matrix products, arithmetic and copies ran while one was open for 6% -> 0% of each run, Pallas kernels for 0% -> 0%
where the time goes in v2:
time: 105 us
  Pallas kernels  97.2 us (93%)
  local copies, waits for them, and re-layouts  6.86 us (7%)
    pallas_call x1, Pallas kernels, local(): pl.pallas_call(kernel, out_shape=[jax.ShapeDtypeStruct((T, D), BF), jax.S...  97.2 us
    unnamed x6, local copies, waits for them, and re-layouts  6.86 us

profile of v2, /device:TPU:96, one launch (start us, length us, event | category | flops | bytes accessed | tf_op | source)
XLA Modules:
  0.0 104.7 jit_solution(16130274949938596562)
XLA Ops:
  0.6 97.2 %shard_map.111 = (bf16[128,1280]{1,0:T(8,128)(2,1)}, bf16[1,128]{1,0:T(2,128)(2,1)}, bf16[1280,640]{1,0:T(8,128)(2,1)}, bf16[640,1280]{1,0:T(8,128)(2,1)}) custom-call(bf16[128,1280]{1,0:T(8,128)(2,1)} %tok_ref.1, bf16[128,1280]{1,0:T(8,128)(2,1)} %grad_ref.1, bf16[1,128]{1,0:T(2,128)(2,1)} %bitcast.12, s32[1,128]{1,0:T(1,128)} %bitcast.13, ...), custom_call_target="tpu_custom_call" | custom-call | flops 12600000512 | bytes 8000000 | tf_op jit(solution)/shard_map/pallas_call | solution.py:393
  97.8 1.7 %copy.16 = bf16[128,1280]{1,0:T(8,128)(2,1)} copy(bf16[128,1280]{1,0:T(8,128)(2,1)} %get-tuple-element.16) | data formatting | bytes 655360
  99.6 1.1 %copy.17 = bf16[128]{0:T(256)(128)(2,1)} copy(bf16[128]{0:T(256)(128)(2,1)} %bitcast.15) | data formatting | bytes 512
  100.7 0.0 copy-start
  100.7 2.9 %copy.18 = bf16[1,1280,640]{2,1,0:T(8,128)(2,1)} copy(bf16[1,1280,640]{2,1,0:T(8,128)(2,1)} %bitcast.9) | data formatting | bytes 3276800
  103.5 0.0 copy-done
  103.5 1.2 %copy.19 = bf16[1,640,1280]{2,1,0:T(8,128)(2,1)} copy(bf16[1,640,1280]{2,1,0:T(8,128)(2,1)S(1)} %bitcast.8) | data formatting | bytes 3276800
Async XLA Ops:
  100.7 2.9 %copy-start = (bf16[640,1280]{1,0:T(8,128)(2,1)S(1)}, bf16[640,1280]{1,0:T(8,128)(2,1)}, u32[]{:S(2)}) copy-start(bf16[640,1280]{1,0:T(8,128)(2,1)} %get-tuple-element.11) | copy-start | bytes 4915204

commit v3 on v2

--- a/solution.py
+++ b/solution.py
@@ -54,10 +54,23 @@
     return far * (2 * (pair % 2) - 1), k % NX
 
 
+def as_column(row):
+    return jnp.broadcast_to(row.astype(F32), (T, T)).T[:, 0:1]
+
+
+def places(ids, z, x):
+    wide = jnp.broadcast_to(ids.astype(F32), (T, T))
+    same = (wide == wide.T) & (iota((T, T), 0) < iota((T, T), 1))
+    slot = jnp.sum(jnp.where(same, 1.0, 0.0), axis=0, keepdims=True).astype(I32)
+    dz = (z - (ids >> 2) + NZ) & (NZ - 1)
+    pair = jnp.where(dz == 0, 0, jnp.where(dz <= NZ // 2, 2 * dz - 1, 2 * (NZ - dz)))
+    return (pair * NX + ((x - (ids & 3) + NX) & (NX - 1))) * 16, slot
+
+
 def kernel(tok_ref, grad_ref, gate_ref, ids_ref, mod_ref, gain_ref, win_hbm, wout_hbm,
-           gtok_ref, ggate_ref, gwin_hbm, gwout_hbm,
-           out_buf, in_buf, rows, win, wout, pre, back, act16, pre16, part, sib, far, near, ret, home,
-           acc_in, acc_out, st_in, st_out, tgt_s,
+           home, gwin_hbm, gwout_hbm,
+           out_buf, in_buf, rows, win, wout, pre, back, act16, pre16, part, sib, far, near, ret,
+           acc_in, acc_out, st_in, st_out,
            w_sem, o_sem, as_sem, ar_sem, gs_sem, gr_sem, rs_sem, rr_sem, bs_sem, br_sem):
     dp, ex = lax.axis_index("dp"), lax.axis_index("expert")
     y, c = dp // 2, dp % 2
@@ -95,17 +108,9 @@
             src_ref=src, dst_ref=dst, send_sem=ssem, recv_sem=rsem, device_id=dev, device_id_type=MESH
         )
 
-    ids = ids_ref[...]
-    wide = jnp.broadcast_to(ids.astype(F32), (T, T))
-    same = (wide == wide.T) & (iota((T, T), 0) < iota((T, T), 1))
-    slot = jnp.sum(jnp.where(same, 1.0, 0.0), axis=0, keepdims=True).astype(I32)
-    tz, tx = ids >> 2, ids & 3
-    dz = (z - tz + NZ) & (NZ - 1)
-    pair = jnp.where(dz == 0, 0, jnp.where(dz <= NZ // 2, 2 * dz - 1, 2 * (NZ - dz)))
-    first = (pair * NX + ((x - tx + NX) & (NX - 1))) * 16
-
-    gate_col = jnp.broadcast_to(gate_ref[...].astype(F32), (T, T)).T[:, 0:1]
-    mod_col = jnp.broadcast_to(mod_ref[...].astype(F32), (T, T)).T[:, 0:1]
+    first, slot = places(ids_ref[...], z, x)
+    gate_col = as_column(gate_ref[...])
+    mod_col = as_column(mod_ref[...])
     gain = jnp.where(mod_col == 1.0, gain_ref[1:2, :], gain_ref[0:1, :])
     tok = tok_ref[...]
     gated = (gate_col * gain * grad_ref[...].astype(F32)).astype(BF)
@@ -128,15 +133,18 @@
     def a2a(k):
         return rdma(out_buf.at[k], in_buf.at[k], as_sem.at[k], ar_sem.at[k], target(k))
 
+    def dispatch(q):
+        @pl.loop(max(1, q * GS), (q + 1) * GS)
+        def _(k):
+            a2a(k).start()
+
     for q in range(Q):
         pack(q)
         if q == 0:
             in_buf[0] = out_buf[0]
             pl.semaphore_wait(barrier, NZ * NX - 1 + 3)
-
-        @pl.loop(max(1, q * GS), (q + 1) * GS)
-        def _(k):
-            a2a(k).start()
+        if q < 2:
+            dispatch(q)
 
     cc = iota((1, GS * 16), 1)
     cs, ci = cc >> 4, cc & 15
@@ -181,6 +189,8 @@
             rows[q, dp, h, :, FW:D] = rest[h * RG:(h + 1) * RG]
         for role in (0, 1, 4):
             gather(q, role).start()
+        if q < 2:
+            dispatch(q + 2)
 
     def second_step(q):
         gather_wait(q, 0)
@@ -205,6 +215,9 @@
     def compute(q):
         for role in range(4, 9):
             gather_wait(q, role)
+        if q == 0:
+            load_in.wait()
+            load_out.wait()
         pre[...] = mm(rows[q, :, 0].reshape(M, D), win[...])
         back[...] = mm_nt(rows[q, :, 1].reshape(M, D), wout[...])
         gates = []
@@ -275,6 +288,8 @@
     def give_back(k):
         return rdma(ret.at[k], home.at[k], bs_sem.at[k], br_sem.at[k], source(k))
 
+    keep = pltpu.make_async_copy(ret.at[0], home.at[0], w_sem.at[2])
+
     def reduce_own(q):
         pair_sum(q, 0).wait_recv()
         total = part[q, dp].astype(F32) + sib[q, 0].astype(F32)
@@ -292,7 +307,7 @@
                 res = jnp.concatenate([res[:, 0:128] + gates, res[:, 128:256]], axis=1)
             ret[q * GS:(q + 1) * GS, :, 256 * h:256 * h + 256] = res.astype(BF).reshape(GS, 16, 256)
         if q == 0:
-            home[0] = ret[0]
+            keep.start()
 
         @pl.loop(max(1, q * GS), (q + 1) * GS)
         def _(k):
@@ -314,61 +329,43 @@
             st_in[...] = (acc_in[...] + gi).astype(BF)
 
     first_step(0)
+    first_step(1)
     second_step(0)
-    first_step(1)
+    first_step(2)
     third_step(0)
-    load_in.wait()
-    load_out.wait()
     second_step(1)
     compute(0)
-    first_step(2)
+    first_step(3)
     third_step(1)
+    second_step(2)
     reduce_far(0)
-    second_step(2)
+    compute(1)
+    third_step(2)
+    second_step(3)
     reduce_near(0)
-    compute(1)
-    first_step(3)
-    third_step(2)
     reduce_far(1)
-    reduce_own(0)
-    second_step(3)
-    reduce_near(1)
     compute(2)
     third_step(3)
+    reduce_near(1)
     reduce_far(2)
+    reduce_own(0)
+    weight_grads(0)
+    compute(3)
+    reduce_near(2)
     reduce_own(1)
-    weight_grads(0)
-    reduce_near(2)
-    compute(3)
     reduce_far(3)
     reduce_own(2)
     reduce_near(3)
     weight_grads(1)
+    reduce_own(3)
     store_in = pltpu.make_async_copy(st_in, gwin_hbm, o_sem.at[0])
     store_out = pltpu.make_async_copy(st_out, gwout_hbm, o_sem.at[1])
     store_in.start()
     store_out.start()
-    reduce_own(3)
 
     @pl.loop(1, NZ * NX)
     def _(k):
         give_back(k).wait_recv()
-
-    tgt_s[...] = jnp.broadcast_to(first.astype(F32), (T, T)).T
-    first_col = tgt_s[:, 0:1].astype(I32)
-    slot_col = jnp.broadcast_to(slot.astype(F32), (T, T)).T[:, 0:1].astype(I32)
-    lanes = iota((T, NZ * NX * 16), 1)
-    back_rows = home[...].reshape(NZ * NX * 16, BW)
-    gtok_ref[:, 0:512] = mm(onehot(lanes == first_col + slot_col), back_rows).astype(BF)
-    gtok_ref[:, 512:1024] = mm(onehot(lanes == first_col + 6 + slot_col), back_rows).astype(BF)
-    low = jnp.where(slot_col < 3, first_col + 12 + slot_col, -1)
-    high = jnp.where(slot_col < 3, -1, first_col + 9 + slot_col)
-    gtok_ref[:, 1024:1280] = (
-        mm(onehot(lanes == low), back_rows[:, 0:256]) + mm(onehot(lanes == high), back_rows[:, 256:512])
-    ).astype(BF)
-    gate_lines = mm(onehot(lanes == first_col + 15), back_rows[:, 0:128])
-    gate_tok = jnp.sum(jnp.where(iota((T, 128), 1) == slot_col, gate_lines, 0.0), axis=1, keepdims=True) / gate_col
-    ggate_ref[...] = jnp.broadcast_to(gate_tok, (T, T)).T[0:1, :].astype(BF)
 
     @pl.loop(1, NZ * NX)
     def _(k):
@@ -382,24 +379,51 @@
             pair_sum(q, j).wait_send()
         for role in range(4):
             ring(q, role).wait_send()
+    keep.wait()
     store_in.wait()
     store_out.wait()
+
+
+def finish(ids_ref, gate_ref, home_hbm, gwin_in, gwout_in, gtok_ref, ggate_ref, gwin_hbm, gwout_hbm, home, sem):
+    copies = [
+        pltpu.make_async_copy(home_hbm, home, sem.at[0]),
+        pltpu.make_async_copy(gwin_in, gwin_hbm, sem.at[1]),
+        pltpu.make_async_copy(gwout_in, gwout_hbm, sem.at[2]),
+    ]
+    for copy in copies:
+        copy.start()
+    ex = lax.axis_index("expert")
+    first, slot = places(ids_ref[...], ex // NX, ex % NX)
+    first, slot = as_column(first).astype(I32), as_column(slot).astype(I32)
+    gate = as_column(gate_ref[...])
+    lanes = iota((T, NZ * NX * 16), 1)
+    copies[0].wait()
+    lines = home[...].reshape(NZ * NX * 16, BW)
+    gtok_ref[:, 0:512] = mm(onehot(lanes == first + slot), lines).astype(BF)
+    gtok_ref[:, 512:1024] = mm(onehot(lanes == first + 6 + slot), lines).astype(BF)
+    low = jnp.where(slot < 3, first + 12 + slot, -1)
+    high = jnp.where(slot < 3, -1, first + 9 + slot)
+    gtok_ref[:, 1024:1280] = (
+        mm(onehot(lanes == low), lines[:, 0:256]) + mm(onehot(lanes == high), lines[:, 256:512])
+    ).astype(BF)
+    gate_lines = mm(onehot(lanes == first + 15), lines[:, 0:128])
+    gate_tok = jnp.sum(jnp.where(iota((T, 128), 1) == slot, gate_lines, 0.0), axis=1, keepdims=True) / gate
+    ggate_ref[...] = jnp.broadcast_to(gate_tok, (T, T)).T[0:1, :].astype(BF)
+    copies[1].wait()
+    copies[2].wait()
 
 
 def local(tokens, grad_out, gate, expert_ids, modality, modal_gain, w_in, w_out):
     vmem = pl.BlockSpec(memory_space=pltpu.VMEM)
     hbm = pl.BlockSpec(memory_space=pl.ANY)
     dma = pltpu.SemaphoreType.DMA
-    grad_tokens, grad_gate, grad_in, grad_out_w = pl.pallas_call(
+    gate_row, ids_row = gate.reshape(1, T), expert_ids.reshape(1, T)
+    weights = [jax.ShapeDtypeStruct((D, F), BF), jax.ShapeDtypeStruct((F, D), BF)]
+    home, in_part, out_part = pl.pallas_call(
         kernel,
-        out_shape=[
-            jax.ShapeDtypeStruct((T, D), BF),
-            jax.ShapeDtypeStruct((1, T), BF),
-            jax.ShapeDtypeStruct((D, F), BF),
-            jax.ShapeDtypeStruct((F, D), BF),
-        ],
+        out_shape=[jax.ShapeDtypeStruct((NZ * NX, 16, BW), BF)] + weights,
         in_specs=[vmem] * 6 + [hbm] * 2,
-        out_specs=[vmem, vmem, hbm, hbm],
+        out_specs=[hbm] * 3,
         scratch_shapes=[
             pltpu.VMEM((NZ * NX, 16, FW), BF),
             pltpu.VMEM((NZ * NX, 16, FW), BF),
@@ -415,13 +439,11 @@
             pltpu.VMEM((Q, 2, 16, CUT), BF),
             pltpu.VMEM((Q, 2, 16, PW), BF),
             pltpu.VMEM((NZ * NX, 16, BW), BF),
-            pltpu.VMEM((NZ * NX, 16, BW), BF),
             pltpu.VMEM((D, F), F32),
             pltpu.VMEM((F, D), F32),
             pltpu.VMEM((D, F), BF),
             pltpu.VMEM((F, D), BF),
-            pltpu.VMEM((T, T), F32),
-            dma((2,)),
+            dma((3,)),
             dma((2,)),
             dma((NZ * NX,)),
             dma((NZ * NX,)),
@@ -439,13 +461,21 @@
     )(
         tokens,
         grad_out,
-        gate.reshape(1, T),
-        expert_ids.reshape(1, T),
+        gate_row,
+        ids_row,
         modality.reshape(1, T),
         modal_gain,
         w_in[0],
         w_out[0],
     )
+    grad_tokens, grad_gate, grad_in, grad_out_w = pl.pallas_call(
+        finish,
+        out_shape=[jax.ShapeDtypeStruct((T, D), BF), jax.ShapeDtypeStruct((1, T), BF)] + weights,
+        in_specs=[vmem] * 2 + [hbm] * 3,
+        out_specs=[vmem] * 2 + [hbm] * 2,
+        scratch_shapes=[pltpu.VMEM((NZ * NX, 16, BW), BF), dma((3,))],
+        compiler_params=pltpu.CompilerParams(vmem_limit_bytes=16 * 1024 * 1024),
+    )(ids_row, gate_row, home, in_part, out_part)
     return grad_tokens, grad_gate.reshape(T), grad_in[None], grad_out_w[None]
 
 

time: 105 us -> 96.9 us (0.923)
  Pallas kernels: 97.2 us -> 92 us
  local copies, waits for them, and re-layouts: 6.86 us -> 3.9 us
    pallas_call x1 -> x2, Pallas kernels: 97.2 us -> 92 us  [the longest x1 89.5 us: local(): pl.pallas_call(kernel, out_shape=[jax.ShapeDtypeStruct((NZ * NX, 16, BW),...]
    unnamed x6 -> x10, local copies, waits for them, and re-layouts: 6.86 us -> 3.9 us
where the time goes in v3:
time: 96.9 us; the launch traced here: 96.7 us
  Pallas kernels  92 us (95%)
  local copies, waits for them, and re-layouts  3.9 us (4%)
    pallas_call x1, Pallas kernels, local(): pl.pallas_call(kernel, out_shape=[jax.ShapeDtypeStruct((NZ * NX, 16, BW),...  89.5 us
    unnamed x10, local copies, waits for them, and re-layouts  3.9 us
    pallas_call x1, Pallas kernels, local(): pl.pallas_call(finish, out_shape=[jax.ShapeDtypeStruct((T, D), BF), jax.S...  2.5 us

profile of v3, /device:TPU:96, one launch (start us, length us, event | category | flops | bytes accessed | tf_op | source)
XLA Modules:
  0.0 96.7 jit_solution(18400105253718106478)
XLA Ops:
  0.6 0.0 copy-start.3
  0.6 0.0 copy-start.4
  0.7 89.5 %shard_map.111 = (bf16[32,16,512]{2,1,0:T(8,128)(2,1)}, bf16[1280,640]{1,0:T(8,128)(2,1)}, bf16[640,1280]{1,0:T(8,128)(2,1)}) custom-call(bf16[128,1280]{1,0:T(8,128)(2,1)} %tok_ref.1, bf16[128,1280]{1,0:T(8,128)(2,1)} %grad_ref.1, bf16[1,128]{1,0:T(2,128)(2,1)} %bitcast.10, s32[1,128]{1,0:T(1,128)} %bitcast.8, s32[1,128]{1,0:T(1,128)} %bitcast.16, ...), custom_call_target="tpu_custom_call" | custom-call | flops 12600000512 | bytes 8000000 | tf_op jit(solution)/shard_map/pallas_call | solution.py:422
  90.1 0.0 copy-done.3
  90.1 0.0 copy-done.4
  90.1 0.0 copy-start
  90.1 1.4 %copy-done = bf16[1280,640]{1,0:T(8,128)(2,1)S(1)} copy-done((bf16[1280,640]{1,0:T(8,128)(2,1)S(1)}, bf16[1280,640]{1,0:T(8,128)(2,1)}, u32[]{:S(2)}) %copy-start) | copy-done | bytes 1638424
  91.6 0.0 copy-start.1
  91.6 1.4 %copy-done.1 = bf16[640,1280]{1,0:T(8,128)(2,1)S(1)} copy-done((bf16[640,1280]{1,0:T(8,128)(2,1)S(1)}, bf16[640,1280]{1,0:T(8,128)(2,1)}, u32[]{:S(2)}) %copy-start.1) | copy-done | bytes 1638424
  93.0 0.0 copy-start.2
  93.0 1.0 %copy-done.2 = bf16[32,16,512]{2,1,0:T(8,128)(2,1)S(1)} copy-done((bf16[32,16,512]{2,1,0:T(8,128)(2,1)S(1)}, bf16[32,16,512]{2,1,0:T(8,128)(2,1)}, u32[]{:S(2)}) %copy-start.2) | copy-done | bytes 524312
  94.0 2.5 %shard_map.112 = (bf16[128,1280]{1,0:T(8,128)(2,1)}, bf16[1,128]{1,0:T(2,128)(2,1)}, bf16[1280,640]{1,0:T(8,128)(2,1)}, bf16[640,1280]{1,0:T(8,128)(2,1)}) custom-call(s32[1,128]{1,0:T(1,128)S(1)} %bitcast.9, bf16[1,128]{1,0:T(2,128)(2,1)S(1)} %bitcast.11, bf16[32,16,512]{2,1,0:T(8,128)(2,1)S(1)} %copy-done.2, bf16[1280,640]{1,0:T(8,128)(2,1)S(1)} %copy-done, ...), custom_call_target="tpu_custom_call" | custom-call | tf_op jit(solution)/shard_map/pallas_call | solution.py:471
Async XLA Ops:
  0.6 89.5 %copy-start.3 = (s32[128,1]{0,1:T(1,128)S(1)}, s32[128,1]{0,1:T(1,128)}, u32[]{:S(2)}) copy-start(s32[128,1]{0,1:T(1,128)} %param.11) | copy-start | bytes 1540
  0.6 89.5 %copy-start.4 = (bf16[128]{0:T(256)(128)(2,1)S(1)}, bf16[128]{0:T(256)(128)(2,1)}, u32[]{:S(2)}) copy-start(bf16[128]{0:T(256)(128)(2,1)} %param.10) | copy-start | bytes 772
  90.1 1.4 %copy-start = (bf16[1280,640]{1,0:T(8,128)(2,1)S(1)}, bf16[1280,640]{1,0:T(8,128)(2,1)}, u32[]{:S(2)}) copy-start(bf16[1280,640]{1,0:T(8,128)(2,1)} %get-tuple-element.12.gwin_in) | copy-start | bytes 4915204
  91.6 1.4 %copy-start.1 = (bf16[640,1280]{1,0:T(8,128)(2,1)S(1)}, bf16[640,1280]{1,0:T(8,128)(2,1)}, u32[]{:S(2)}) copy-start(bf16[640,1280]{1,0:T(8,128)(2,1)} %get-tuple-element.13.gwout_in) | copy-start | bytes 4915204
  93.0 1.0 %copy-start.2 = (bf16[32,16,512]{2,1,0:T(8,128)(2,1)S(1)}, bf16[32,16,512]{2,1,0:T(8,128)(2,1)}, u32[]{:S(2)}) copy-start(bf16[32,16,512]{2,1,0:T(8,128)(2,1)} %get-tuple-element.11.home_hbm) | copy-start | bytes 1572868

commit v4 on v3

--- a/solution.py
+++ b/solution.py
@@ -357,11 +357,11 @@
     reduce_own(2)
     reduce_near(3)
     weight_grads(1)
-    reduce_own(3)
     store_in = pltpu.make_async_copy(st_in, gwin_hbm, o_sem.at[0])
     store_out = pltpu.make_async_copy(st_out, gwout_hbm, o_sem.at[1])
     store_in.start()
     store_out.start()
+    reduce_own(3)
 
     @pl.loop(1, NZ * NX)
     def _(k):
@@ -421,7 +421,7 @@
     weights = [jax.ShapeDtypeStruct((D, F), BF), jax.ShapeDtypeStruct((F, D), BF)]
     home, in_part, out_part = pl.pallas_call(
         kernel,
-        out_shape=[jax.ShapeDtypeStruct((NZ * NX, 16, BW), BF)] + weights,
+        out_shape=[pltpu.VMEM((NZ * NX, 16, BW), BF), pltpu.VMEM((D, F), BF), pltpu.VMEM((F, D), BF)],
         in_specs=[vmem] * 6 + [hbm] * 2,
         out_specs=[hbm] * 3,
         scratch_shapes=[

time: 96.9 us -> 92.5 us (0.955)
  local copies, waits for them, and re-layouts: 3.9 us -> 0.01 us
    unnamed x10 -> x4, local copies, waits for them, and re-layouts: 3.9 us -> 0.01 us
where the time goes in v4:
time: 92.5 us; the launch traced here: 92.1 us
  Pallas kernels  91.2 us (99%)
    pallas_call x1, Pallas kernels, local(): pl.pallas_call(kernel, out_shape=[pltpu.VMEM((NZ * NX, 16, BW), BF), pltp...  88.7 us
    pallas_call x1, Pallas kernels, local(): pl.pallas_call(finish, out_shape=[jax.ShapeDtypeStruct((T, D), BF), jax.S...  2.5 us

profile of v4, /device:TPU:96, one launch (start us, length us, event | category | flops | bytes accessed | tf_op | source)
XLA Modules:
  0.0 92.1 jit_solution(17577307761338049302)
XLA Ops:
  0.6 0.0 copy-start
  0.6 0.0 copy-start.1
  0.7 88.7 %shard_map.111 = (bf16[32,16,512]{2,1,0:T(8,128)(2,1)S(1)}, bf16[1280,640]{1,0:T(8,128)(2,1)S(1)}, bf16[640,1280]{1,0:T(8,128)(2,1)S(1)}) custom-call(bf16[128,1280]{1,0:T(8,128)(2,1)} %tok_ref.1, bf16[128,1280]{1,0:T(8,128)(2,1)} %grad_ref.1, bf16[1,128]{1,0:T(2,128)(2,1)} %bitcast.10, s32[1,128]{1,0:T(1,128)} %bitcast.8, s32[1,128]{1,0:T(1,128)} %bitcast.16, ...), custom_call_target="tpu_custom_call" | custom-call | flops 12600000512 | bytes 8000000 | tf_op jit(solution)/shard_map/pallas_call | solution.py:422
  89.4 0.0 copy-done
  89.4 0.0 copy-done.1
  89.4 2.5 %shard_map.112 = (bf16[128,1280]{1,0:T(8,128)(2,1)}, bf16[1,128]{1,0:T(2,128)(2,1)}, bf16[1280,640]{1,0:T(8,128)(2,1)}, bf16[640,1280]{1,0:T(8,128)(2,1)}) custom-call(s32[1,128]{1,0:T(1,128)S(1)} %bitcast.9, bf16[1,128]{1,0:T(2,128)(2,1)S(1)} %bitcast.11, bf16[32,16,512]{2,1,0:T(8,128)(2,1)S(1)} %get-tuple-element.11.home_hbm, ...), custom_call_target="tpu_custom_call" | custom-call | tf_op jit(solution)/shard_map/pallas_call | solution.py:471
Async XLA Ops:
  0.6 88.7 %copy-start = (s32[128,1]{0,1:T(1,128)S(1)}, s32[128,1]{0,1:T(1,128)}, u32[]{:S(2)}) copy-start(s32[128,1]{0,1:T(1,128)} %param.11) | copy-start | bytes 1540
  0.6 88.7 %copy-start.1 = (bf16[128]{0:T(256)(128)(2,1)S(1)}, bf16[128]{0:T(256)(128)(2,1)}, u32[]{:S(2)}) copy-start(bf16[128]{0:T(256)(128)(2,1)} %param.10) | copy-start | bytes 772

commit v5 on v4

--- a/solution.py
+++ b/solution.py
@@ -49,7 +49,9 @@
 
 
 def offset(k):
-    pair = k // NX
+    group = k // GS
+    group += (group + 3) // 4 - 3 * (group // 3)
+    pair = 2 * group + k // NX % 2
     far = (pair + 1) // 2
     return far * (2 * (pair % 2) - 1), k % NX
 
@@ -64,6 +66,9 @@
     slot = jnp.sum(jnp.where(same, 1.0, 0.0), axis=0, keepdims=True).astype(I32)
     dz = (z - (ids >> 2) + NZ) & (NZ - 1)
     pair = jnp.where(dz == 0, 0, jnp.where(dz <= NZ // 2, 2 * dz - 1, 2 * (NZ - dz)))
+    group = pair >> 1
+    group = jnp.where(group == 0, 0, jnp.where(group == 1, 3, group - 1))
+    pair = 2 * group + (pair & 1)
     return (pair * NX + ((x - (ids & 3) + NX) & (NX - 1))) * 16, slot
 
 
@@ -236,7 +241,7 @@
         tokens = mm_nt(pre16[q], win[...]).astype(BF).reshape(8, 3, 16, D)
         for g in range(3):
             part[q, :, :, g * D:(g + 1) * D] = tokens[:, g]
-        for j in range(NY):
+        for j in (2, 1, 3, 0):
             pair_sum(q, j).start()
 
     def pair_sum(q, j):
@@ -340,27 +345,27 @@
     second_step(2)
     reduce_far(0)
     compute(1)
+    second_step(3)
     third_step(2)
-    second_step(3)
     reduce_near(0)
     reduce_far(1)
     compute(2)
     third_step(3)
+    reduce_far(2)
+    compute(3)
     reduce_near(1)
-    reduce_far(2)
+    reduce_far(3)
     reduce_own(0)
+    reduce_near(2)
     weight_grads(0)
-    compute(3)
-    reduce_near(2)
     reduce_own(1)
-    reduce_far(3)
-    reduce_own(2)
     reduce_near(3)
     weight_grads(1)
     store_in = pltpu.make_async_copy(st_in, gwin_hbm, o_sem.at[0])
     store_out = pltpu.make_async_copy(st_out, gwout_hbm, o_sem.at[1])
     store_in.start()
     store_out.start()
+    reduce_own(2)
     reduce_own(3)
 
     @pl.loop(1, NZ * NX)

time: 92.5 us -> 90.2 us (0.975)
  Pallas kernels: 91.2 us -> 88.5 us
    pallas_call x1, Pallas kernels: 88.7 us -> 86 us  [local(): pl.pallas_call(kernel, out_shape=[pltpu.VMEM((NZ * NX, 16, BW), BF), pltp...]
where the time goes in v5:
time: 90.2 us; the launch traced here: 89.3 us
  Pallas kernels  88.5 us (98%)
    pallas_call x1, Pallas kernels, local(): pl.pallas_call(kernel, out_shape=[pltpu.VMEM((NZ * NX, 16, BW), BF), pltp...  86 us
    pallas_call x1, Pallas kernels, local(): pl.pallas_call(finish, out_shape=[jax.ShapeDtypeStruct((T, D), BF), jax.S...  2.5 us

profile of v5, /device:TPU:96, one launch (start us, length us, event | category | flops | bytes accessed | tf_op | source)
XLA Modules:
  0.0 89.3 jit_solution(14752242448084006916)
XLA Ops:
  0.6 0.0 copy-start
  0.6 0.0 copy-start.1
  0.7 86.0 %shard_map.111 = (bf16[32,16,512]{2,1,0:T(8,128)(2,1)S(1)}, bf16[1280,640]{1,0:T(8,128)(2,1)S(1)}, bf16[640,1280]{1,0:T(8,128)(2,1)S(1)}) custom-call(bf16[128,1280]{1,0:T(8,128)(2,1)} %tok_ref.1, bf16[128,1280]{1,0:T(8,128)(2,1)} %grad_ref.1, bf16[1,128]{1,0:T(2,128)(2,1)} %bitcast.10, s32[1,128]{1,0:T(1,128)} %bitcast.8, s32[1,128]{1,0:T(1,128)} %bitcast.16, ...), custom_call_target="tpu_custom_call" | custom-call | flops 12600000512 | bytes 8000000 | tf_op jit(solution)/shard_map/pallas_call | solution.py:427
  86.6 0.0 copy-done
  86.6 0.0 copy-done.1
  86.6 2.5 %shard_map.112 = (bf16[128,1280]{1,0:T(8,128)(2,1)}, bf16[1,128]{1,0:T(2,128)(2,1)}, bf16[1280,640]{1,0:T(8,128)(2,1)}, bf16[640,1280]{1,0:T(8,128)(2,1)}) custom-call(s32[1,128]{1,0:T(1,128)S(1)} %bitcast.9, bf16[1,128]{1,0:T(2,128)(2,1)S(1)} %bitcast.11, bf16[32,16,512]{2,1,0:T(8,128)(2,1)S(1)} %get-tuple-element.11.home_hbm, ...), custom_call_target="tpu_custom_call" | custom-call | tf_op jit(solution)/shard_map/pallas_call | solution.py:476
Async XLA Ops:
  0.6 86.0 %copy-start = (s32[128,1]{0,1:T(1,128)S(1)}, s32[128,1]{0,1:T(1,128)}, u32[]{:S(2)}) copy-start(s32[128,1]{0,1:T(1,128)} %param.11) | copy-start | bytes 1540
  0.6 86.0 %copy-start.1 = (bf16[128]{0:T(256)(128)(2,1)S(1)}, bf16[128]{0:T(256)(128)(2,1)}, u32[]{:S(2)}) copy-start(bf16[128]{0:T(256)(128)(2,1)} %param.10) | copy-start | bytes 772

commit v6 on v5

--- a/solution.py
+++ b/solution.py
@@ -360,12 +360,12 @@
     weight_grads(0)
     reduce_own(1)
     reduce_near(3)
+    reduce_own(2)
     weight_grads(1)
     store_in = pltpu.make_async_copy(st_in, gwin_hbm, o_sem.at[0])
     store_out = pltpu.make_async_copy(st_out, gwout_hbm, o_sem.at[1])
     store_in.start()
     store_out.start()
-    reduce_own(2)
     reduce_own(3)
 
     @pl.loop(1, NZ * NX)

time: 90.2 us -> 90 us (level)
  no operation moved by 1% of the time
where the time goes in v6:
time: 90 us; the launch traced here: 88.8 us
  Pallas kernels  87.9 us (98%)
    pallas_call x1, Pallas kernels, local(): pl.pallas_call(kernel, out_shape=[pltpu.VMEM((NZ * NX, 16, BW), BF), pltp...  85.4 us
    pallas_call x1, Pallas kernels, local(): pl.pallas_call(finish, out_shape=[jax.ShapeDtypeStruct((T, D), BF), jax.S...  2.5 us

profile of v6, /device:TPU:96, one launch (start us, length us, event | category | flops | bytes accessed | tf_op | source)
XLA Modules:
  0.0 88.8 jit_solution(740679913525638689)
XLA Ops:
  0.6 0.0 copy-start
  0.6 0.0 copy-start.1
  0.7 85.4 %shard_map.111 = (bf16[32,16,512]{2,1,0:T(8,128)(2,1)S(1)}, bf16[1280,640]{1,0:T(8,128)(2,1)S(1)}, bf16[640,1280]{1,0:T(8,128)(2,1)S(1)}) custom-call(bf16[128,1280]{1,0:T(8,128)(2,1)} %tok_ref.1, bf16[128,1280]{1,0:T(8,128)(2,1)} %grad_ref.1, bf16[1,128]{1,0:T(2,128)(2,1)} %bitcast.10, s32[1,128]{1,0:T(1,128)} %bitcast.8, s32[1,128]{1,0:T(1,128)} %bitcast.16, ...), custom_call_target="tpu_custom_call" | custom-call | flops 12600000512 | bytes 8000000 | tf_op jit(solution)/shard_map/pallas_call | solution.py:427
  86.1 0.0 copy-done
  86.1 0.0 copy-done.1
  86.1 2.5 %shard_map.112 = (bf16[128,1280]{1,0:T(8,128)(2,1)}, bf16[1,128]{1,0:T(2,128)(2,1)}, bf16[1280,640]{1,0:T(8,128)(2,1)}, bf16[640,1280]{1,0:T(8,128)(2,1)}) custom-call(s32[1,128]{1,0:T(1,128)S(1)} %bitcast.9, bf16[1,128]{1,0:T(2,128)(2,1)S(1)} %bitcast.11, bf16[32,16,512]{2,1,0:T(8,128)(2,1)S(1)} %get-tuple-element.11.home_hbm, ...), custom_call_target="tpu_custom_call" | custom-call | tf_op jit(solution)/shard_map/pallas_call | solution.py:476
Async XLA Ops:
  0.6 85.5 %copy-start = (s32[128,1]{0,1:T(1,128)S(1)}, s32[128,1]{0,1:T(1,128)}, u32[]{:S(2)}) copy-start(s32[128,1]{0,1:T(1,128)} %param.11) | copy-start | bytes 1540
  0.6 85.5 %copy-start.1 = (bf16[128]{0:T(256)(128)(2,1)S(1)}, bf16[128]{0:T(256)(128)(2,1)}, u32[]{:S(2)}) copy-start(bf16[128]{0:T(256)(128)(2,1)} %param.10) | copy-start | bytes 772
